TPU v7x, 256 devices: a whole 4x4x8 slice. The times are simulated.
256 devices in a mesh: dp: 2 (over z_lo), seq: 128 (over x, z_hi, y, core).
Axes of the slice: x: 4, y: 4, z: 8 (z_hi: 4, z_lo: 2; z = z_hi * 2 + z_lo), core: 2. Of those that a mesh axis runs over, the one named last changes fastest.
Arguments:
- frames: bfloat16 [2, 32768, 256], P('dp', 'seq'), may hold values from -6 to 6
- upstream: bfloat16 [2, 256, 256, 256], P('dp', 'seq'), may hold values from -6 to 6
- intra_weights: bfloat16 [4, 256, 256], replicated, may hold values from -0.375 to 0.375
- inter_weights: bfloat16 [4, 256, 256], replicated, may hold values from -0.375 to 0.375
- gains: float32 [2, 256], replicated, may hold values from 0.5 to 1.5
Outputs:
- grad_frames: bfloat16 [2, 32768, 256], P('dp', 'seq')
- grad_intra: float32 [4, 256, 256], replicated
- grad_inter: float32 [4, 256, 256], replicated
- grad_gains: float32 [2, 256], replicated
All inputs are finite; a program needn't handle non-finite values.
Results may differ from a plain program's by a relative error of at most 0.025.
Values may be sent and summed in bfloat16 or wider, within the bound.
A program may use at most 64 MiB of HBM per device.

v0:
```python
import jax
import jax.numpy as jnp
from jax import lax
from jax.sharding import PartitionSpec as P

H = 8
K = 256


epsilon = 1e-05


def shifted(block, axis, distance):
    devices = range(lax.axis_size(axis))
    route = [(i - distance, i) for i in devices if i - distance in devices]
    return lax.ppermute(block, axis, route)


def product(form, left, right):
    return jnp.einsum(form, left, right, preferred_element_type=jnp.float32)


def layer_forward(source, matrices, scaling):
    groups, length, width = source.shape
    head_size = width // H
    values_f = source.astype(jnp.float32)
    centred = values_f - jnp.mean(values_f, -1, keepdims=True)
    inverse = lax.rsqrt(jnp.mean(centred * centred, -1, keepdims=True) + epsilon)
    normed = centred * inverse
    hidden = (normed * scaling).astype(jnp.bfloat16)
    projected = product("gln,cnm->cglm", hidden, matrices[:3]).astype(jnp.bfloat16)
    queries = projected[0].reshape(groups, length, H, head_size)
    key_rows = projected[1].reshape(groups, length, H, head_size)
    value_rows = projected[2].reshape(groups, length, H, head_size)
    scores = product("glhd,gmhd->ghlm", queries, key_rows) * head_size ** (-0.5)
    attend = jax.nn.softmax(scores, axis=-1)
    rounded = attend.astype(jnp.bfloat16)
    combined = (
        product("ghlm,gmhd->glhd", rounded, value_rows)
        .astype(jnp.bfloat16)
        .reshape(groups, length, width)
    )
    result = values_f + product("gln,nm->glm", combined, matrices[3])
    saved = (normed, inverse, hidden, queries, key_rows, value_rows, rounded, attend, combined)
    return (result, saved)


def layer_backward(saved, upstream, matrices, scaling):
    normed, inverse, hidden, queries, key_rows, value_rows, rounded, attend, combined = saved
    groups, length, width = upstream.shape
    head_size = width // H
    grad_out = product("gln,glm->nm", combined, upstream)
    grad_comb = (
        product("glm,nm->gln", upstream, matrices[3])
        .astype(jnp.bfloat16)
        .reshape(groups, length, H, head_size)
    )
    grad_attend = product("glhd,gmhd->ghlm", grad_comb, value_rows)
    grad_values = product("ghlm,glhd->gmhd", rounded, grad_comb).astype(jnp.bfloat16)
    grad_scores = (
        attend
        * (grad_attend - jnp.sum(grad_attend * attend, -1, keepdims=True))
        * head_size ** (-0.5)
    ).astype(jnp.bfloat16)
    grad_queries = product("ghlm,gmhd->glhd", grad_scores, key_rows).astype(jnp.bfloat16)
    grad_keys = product("ghlm,glhd->gmhd", grad_scores, queries).astype(jnp.bfloat16)
    grad_proj = jnp.stack([grad_queries, grad_keys, grad_values]).reshape(3, groups, length, width)
    grad_mats = product("gln,cglm->cnm", hidden, grad_proj)
    grad_hidden = product("cglm,cnm->gln", grad_proj, matrices[:3])
    grad_gain = jnp.sum(grad_hidden * normed, axis=(0, 1))
    grad_normed = grad_hidden * scaling
    grad_norm = inverse * (
        grad_normed
        - jnp.mean(grad_normed, -1, keepdims=True)
        - normed * jnp.mean(grad_normed * normed, -1, keepdims=True)
    )
    grad_source = upstream.astype(jnp.float32) + grad_norm
    return (grad_source, jnp.concatenate([grad_mats, grad_out[None]], 0), grad_gain)


def send_tail(second_last):
    return shifted(second_last.astype(jnp.bfloat16), "seq", 1).astype(second_last.dtype)


def on_device(frames, upstream, intra_weights, inter_weights, gains):
    mixtures, frame_count, width = frames.shape
    hop_size = K // 2
    span_count = frame_count // hop_size
    seq_devices = lax.axis_size("seq")
    positions = K // seq_devices
    pieces = frames.reshape(mixtures, span_count, hop_size, width)
    following = shifted(pieces[:, 0], "seq", -1)
    later = jnp.concatenate([pieces[:, 1:], following[:, None]], axis=1)
    spans = jnp.concatenate([pieces, later], axis=2).reshape(mixtures * span_count, K, width)
    inner_out, saved = layer_forward(spans, intra_weights, gains[0])
    inner = (
        inner_out.astype(jnp.bfloat16).reshape(mixtures, span_count, K, width).transpose(0, 2, 1, 3)
    )
    inner = inner.reshape(mixtures, seq_devices, positions, span_count, width)
    by_position = lax.all_to_all(inner, "seq", split_axis=1, concat_axis=3, tiled=True)
    by_position = by_position.reshape(mixtures * positions, seq_devices * span_count, width)
    upper = upstream.reshape(mixtures * positions, seq_devices * span_count, width)

    def inter_step(totals, inputs):
        source, grad_top = inputs
        result, kept = layer_forward(source[None], inter_weights, gains[1])
        grad_source, grad_mats, grad_gain = layer_backward(
            kept, grad_top[None], inter_weights, gains[1]
        )
        return ((totals[0] + grad_mats, totals[1] + grad_gain), grad_source[0].astype(jnp.bfloat16))

    start = (jnp.zeros((4, width, width), jnp.float32), jnp.zeros((width,), jnp.float32))
    (grad_inter, gain_inter), grad_inner = lax.scan(inter_step, start, (by_position, upper))
    grad_inner = grad_inner.reshape(mixtures, positions, seq_devices, span_count, width)
    returned = lax.all_to_all(grad_inner, "seq", split_axis=2, concat_axis=1, tiled=True)
    returned = returned.reshape(mixtures, K, span_count, width).transpose(0, 2, 1, 3)
    grad_flat, grad_intra, gain_intra = layer_backward(
        saved, returned.reshape(-1, K, width), intra_weights, gains[0]
    )
    grad_spans = grad_flat.reshape(mixtures, span_count, K, width)
    carried = send_tail(grad_spans[:, -1, hop_size:])
    second_half = grad_spans[:, :, hop_size:]
    previous = jnp.concatenate([carried[:, None], second_half[:, :-1]], axis=1)
    grad_frames = (
        (grad_spans[:, :, :hop_size] + previous)
        .reshape(mixtures, frame_count, width)
        .astype(jnp.bfloat16)
    )
    grad_intra, grad_inter, gain_intra, gain_inter = lax.psum(
        (grad_intra, grad_inter, gain_intra, gain_inter), ("dp", "seq")
    )
    return (grad_frames, grad_intra, grad_inter, jnp.stack([gain_intra, gain_inter]))


def solution(mesh):
    placed = (P("dp", "seq", None), P("dp", "seq", None, None), P(), P(), P())
    return jax.shard_map(
        on_device,
        mesh=mesh,
        in_specs=placed,
        out_specs=(P("dp", "seq", None), P(), P(), P()),
        check_vma=False,
    )
```

profile of v0, /device:TPU:1, one launch (start us, length us, event | category | flops | bytes accessed | tf_op | source)
XLA Modules:
  0.0 433.1 jit_solution(9440357860390155640)
XLA Ops:
  8.1 5.1 %collective-permute-start = (bf16[1,128,256]{2,1,0:T(8,128)(2,1)S(1)}, bf16[1,128,256]{2,1,0:T(8,128)(2,1)S(1)}, u32[]{:S(2)}, u32[]{:S(2)}) collective-permute-start(bf16[1,128,256]{2,1,0:T(8,128)(2,1)S(1)} %get-tuple-element.151), channel_id=1, source_target_pairs={{1,0},{2,1},{3,2},{4,3},{5,4},{6,5},{7,6},{8,7},{9,8},{10,9},{11,1... | collective-permute-start | bytes 196616 | tf_op jit(solution)/shard_map/ppermute | solution.py:16
  18.6 3.4 fusion.153
  22.1 2.7 convolution_convert_fusion.7
  27.2 19.6 %all-to-all-start = ((bf16[1,128,2,2,256]{4,2,3,0,1:T(2,128)(2,1)}), bf16[1,128,2,2,256]{4,2,3,0,1:T(2,128)(2,1)S(1)}, u32[]{:S(2)}, u32[]{:S(2)}) async-start(bf16[1,128,2,2,256]{4,2,3,0,1:T(2,128)(2,1)} %copy.92), calls=%async_computation | async-start | bytes 524288 | tf_op jit(solution)/shard_map/all_to_all | solution.py:100
  48.7 12.8 %all-to-all-done = bf16[1,128,2,2,256]{4,2,3,0,1:T(2,128)(2,1)S(1)} async-done(((bf16[1,128,2,2,256]{4,2,3,0,1:T(2,128)(2,1)}), bf16[1,128,2,2,256]{4,2,3,0,1:T(2,128)(2,1)S(1)}, u32[]{:S(2)}, u32[]{:S(2)}) %all-to-all-start) | async-done | bytes 262176 | tf_op jit(solution)/shard_map/all_to_all | solution.py:100
  61.7 58.4 %while.15 = (s32[]{:T(128)}, f32[4,256,256]{1,2,0:T(8,128)S(1)}, f32[256]{0:T(256)S(1)}, bf16[2,256,256]{1,2,0:T(8,128)(2,1)}, bf16[2,256,256]{1,2,0:T(8,128)(2,...) while((s32[]{:T(128)}, f32[4,256,256]{1,2,0:T(8,128)S(1)}, ...), condition=%wide.region_13.14_spmd.clone, body=%wide.region_4.13_spmd.clone.sunk | while | flops 655173376 | bytes 29698392 | solution.py:113
  66.9 3.7 fusion.244
  70.7 2.7 convolution_convert_fusion.13
  73.3 2.7 convolution_convert_fusion.11
  76.1 3.6 fusion.247
  79.7 3.6 fusion.246
  96.1 3.7 fusion.244
  99.9 2.7 convolution_convert_fusion.13
  102.6 2.7 convolution_convert_fusion.11
  105.3 3.6 fusion.247
  108.9 3.6 fusion.246
  122.0 6.9 %all-to-all-start.1 = ((bf16[1,2,128,2,256]{4,1,3,0,2:T(2,128)(2,1)}), bf16[1,2,128,2,256]{4,1,3,0,2:T(2,128)(2,1)S(1)}, u32[]{:S(2)}, u32[]{:S(2)}) async-start(bf16[1,2,128,2,256]{4,1,3,0,2:T(2,128)(2,1)} %bitcast.23), calls=%async_computation.1 | async-start | bytes 524288 | tf_op jit(solution)/shard_map/all_to_all | solution.py:115
  130.3 13.8 %all-to-all-done.1 = bf16[1,2,128,2,256]{4,1,3,0,2:T(2,128)(2,1)S(1)} async-done(((bf16[1,2,128,2,256]{4,1,3,0,2:T(2,128)(2,1)}), bf16[1,2,128,2,256]{4,1,3,0,2:T(2,128)(2,1)S(1)}, u32[]{:S(2)}, u32[]{:S(2)}) %all-to-all-start.1) | async-done | bytes 262176 | tf_op jit(solution)/shard_map/all_to_all | solution.py:115
  145.0 3.0 convolution_convert_fusion.5
  148.0 2.7 fusion.155
  150.8 7.1 %fusion.100 = bf16[2,8,32,256]{3,2,1,0:T(8,128)(2,1)S(1)} fusion(bf16[2,256,8,32]{1,3,2,0:T(8,128)(2,1)S(1)} %bitcast.372, f32[2,8,256,256]{2,3,1,0:T(8,128)} %fusion.155, f32[2,8,256,256]{2,3,1,0:T(8,128)} %get-tuple-element.153, f32[2,8,256]{2,1,0:T(8,128)S(1)} %copy-done.32), kind=kOutput, calls=%fused_computation.101 | convolution fusion | flops 74584320 | bytes 8929280 | tf_op jit(solution)/shard_map/ghlm,gmhd->glhd/dot_general | solution.py:20
  158.0 7.1 %fusion.103 = bf16[2,8,32,256]{3,2,1,0:T(8,128)(2,1)S(1)} fusion(bf16[2,256,8,32]{1,3,2,0:T(8,128)(2,1)S(1)} %bitcast.370, f32[2,8,256,256]{2,3,1,0:T(8,128)} %fusion.155, f32[2,8,256,256]{2,3,1,0:T(8,128)} %get-tuple-element.153, f32[2,8,256]{2,1,0:T(8,128)S(1)} %copy-done.32), kind=kOutput, calls=%fused_computation.102 | convolution fusion | flops 74584320 | bytes 8929280 | tf_op jit(solution)/shard_map/ghlm,glhd->gmhd/dot_general | solution.py:20
  170.7 77.3 %all-reduce = (f32[1,256]{1,0:T(1,128)S(1)}, f32[1,256]{1,0:T(1,128)S(1)}) all-reduce(f32[1,256]{1,0:T(1,128)S(1)} %bitcast.374, f32[1,256]{1,0:T(1,128)S(1)} %bitcast.379), channel_id=1, replica_groups=mesh['dp'=2,'seq'=128] {'dp','seq'}, use_global_device_ids=true, to_apply=%region_21.22 | all-reduce | flops 512 | bytes 4096 | tf_op jit(solution)/shard_map/psum | solution.py:129
  249.3 173.3 %all-reduce.4.cloned.1.call-done = (f32[4,256,256]{1,2,0:T(8,128)}, f32[4,256,256]{2,1,0:T(8,128)}) async-done(((f32[4,256,256]{1,2,0:T(8,128)}, f32[4,256,256]{2,1,0:T(8,128)}), (f32[4,256,256]{1,2,0:T(8,128)}, f32[4,256,256]{2,1,0:T(8,128)})) %all-reduce.4.cloned.1.call-update) | async-done | bytes 2097168 | tf_op jit(solution)/shard_map/psum | solution.py:129
  (163 shorter events, 50.4 us)
Async XLA Ops:
  8.1 16.8 %copy-start.10 = (bf16[1,1,128,256]{3,2,1,0:T(8,128)(2,1)}, bf16[1,1,128,256]{3,2,1,0:T(8,128)(2,1)S(1)}, u32[]{:S(2)}) copy-start(bf16[1,1,128,256]{3,2,1,0:T(8,128)(2,1)S(1)} %get-tuple-element.150) | copy-start | bytes 196612
  8.1 6.5 %collective-permute-start = (bf16[1,128,256]{2,1,0:T(8,128)(2,1)S(1)}, bf16[1,128,256]{2,1,0:T(8,128)(2,1)S(1)}, u32[]{:S(2)}, u32[]{:S(2)}) collective-permute-start(bf16[1,128,256]{2,1,0:T(8,128)(2,1)S(1)} %get-tuple-element.151), channel_id=1, source_target_pairs={{1,0},{2,1},{3,2},{4,3},{5,4},{6,5},{7,6},{8,7},{9,8},{10,9},{11,1... | collective-permute-start | bytes 196616 | tf_op jit(solution)/shard_map/ppermute | solution.py:16
  14.6 10.3 %copy-start.12 = (bf16[1,128,256]{2,1,0:T(8,128)(2,1)}, bf16[1,128,256]{2,1,0:T(8,128)(2,1)S(1)}, u32[]{:S(2)}) copy-start(bf16[1,128,256]{2,1,0:T(8,128)(2,1)S(1)} %collective-permute-done) | copy-start | bytes 196612
  24.8 22.0 %copy-start.15 = (bf16[2,8,32,256]{3,2,1,0:T(8,128)(2,1)}, bf16[2,8,32,256]{3,2,1,0:T(8,128)(2,1)S(1)}, u32[]{:S(2)}) copy-start(bf16[2,8,32,256]{3,2,1,0:T(8,128)(2,1)S(1)} %convolution_convert_fusion.7) | copy-start | bytes 786436
  24.8 22.0 %copy-start.17 = (bf16[1,2,256,256]{3,2,1,0:T(8,128)(2,1)S(1)}, bf16[1,2,256,256]{3,2,1,0:T(8,128)(2,1)}, u32[]{:S(2)}) copy-start(bf16[1,2,256,256]{3,2,1,0:T(8,128)(2,1)} %param.8) | copy-start | bytes 786436
  24.8 22.9 %copy-start.14 = (bf16[4,256,256]{2,1,0:T(8,128)(2,1)S(1)}, bf16[4,256,256]{2,1,0:T(8,128)(2,1)}, u32[]{:S(2)}) copy-start(bf16[4,256,256]{2,1,0:T(8,128)(2,1)} %param.10) | copy-start | bytes 1572868
  27.2 34.3 %all-to-all-start = ((bf16[1,128,2,2,256]{4,2,3,0,1:T(2,128)(2,1)}), bf16[1,128,2,2,256]{4,2,3,0,1:T(2,128)(2,1)S(1)}, u32[]{:S(2)}, u32[]{:S(2)}) async-start(bf16[1,128,2,2,256]{4,2,3,0,1:T(2,128)(2,1)} %copy.92), calls=%async_computation | async-start | bytes 524288 | tf_op jit(solution)/shard_map/all_to_all | solution.py:100
  83.3 6.9 %copy-start.2 = (bf16[8,32,256]{2,1,0:T(8,128)(2,1)S(1)}, bf16[8,32,256]{2,1,0:T(8,128)(2,1)}, u32[]{:S(2)}) copy-start(bf16[8,32,256]{2,1,0:T(8,128)(2,1)} %fusion.247) | copy-start | bytes 393220 | tf_op jit(solution)/shard_map/while
  83.3 6.9 %copy-start.3 = (bf16[8,32,256]{2,1,0:T(8,128)(2,1)S(1)}, bf16[8,32,256]{2,1,0:T(8,128)(2,1)}, u32[]{:S(2)}) copy-start(bf16[8,32,256]{2,1,0:T(8,128)(2,1)} %fusion.246) | copy-start | bytes 393220 | tf_op jit(solution)/shard_map/while
  112.5 6.9 %copy-start.2 = (bf16[8,32,256]{2,1,0:T(8,128)(2,1)S(1)}, bf16[8,32,256]{2,1,0:T(8,128)(2,1)}, u32[]{:S(2)}) copy-start(bf16[8,32,256]{2,1,0:T(8,128)(2,1)} %fusion.247) | copy-start | bytes 393220 | tf_op jit(solution)/shard_map/while
  112.5 6.9 %copy-start.3 = (bf16[8,32,256]{2,1,0:T(8,128)(2,1)S(1)}, bf16[8,32,256]{2,1,0:T(8,128)(2,1)}, u32[]{:S(2)}) copy-start(bf16[8,32,256]{2,1,0:T(8,128)(2,1)} %fusion.246) | copy-start | bytes 393220 | tf_op jit(solution)/shard_map/while
  120.1 24.3 %copy-start.16 = (bf16[2,8,32,256]{3,2,1,0:T(8,128)(2,1)S(1)}, bf16[2,8,32,256]{3,2,1,0:T(8,128)(2,1)}, u32[]{:S(2)}) copy-start(bf16[2,8,32,256]{3,2,1,0:T(8,128)(2,1)} %copy-done.15) | copy-start | bytes 786436
  122.0 22.2 %all-to-all-start.1 = ((bf16[1,2,128,2,256]{4,1,3,0,2:T(2,128)(2,1)}), bf16[1,2,128,2,256]{4,1,3,0,2:T(2,128)(2,1)S(1)}, u32[]{:S(2)}, u32[]{:S(2)}) async-start(bf16[1,2,128,2,256]{4,1,3,0,2:T(2,128)(2,1)} %bitcast.23), calls=%async_computation.1 | async-start | bytes 524288 | tf_op jit(solution)/shard_map/all_to_all | solution.py:115
  128.9 15.8 %copy-start.24 = (bf16[4,256,256]{2,1,0:T(8,128)(2,1)S(1)}, bf16[4,256,256]{2,1,0:T(8,128)(2,1)}, u32[]{:S(2)}) copy-start(bf16[4,256,256]{2,1,0:T(8,128)(2,1)} %param.9) | copy-start | bytes 1572868
  129.0 293.7 %all-reduce.4.cloned.1.call-start = ((), (), s32[]{:S(2)}) async-start(), calls=%async_computation.2 | async-start | bytes 4194304 | tf_op jit(solution)/shard_map/psum | solution.py:129
  129.0 16.0 %copy-start.32 = (f32[2,8,256]{2,1,0:T(8,128)S(1)}, f32[2,8,256]{2,1,0:T(8,128)}, u32[]{:S(2)}) copy-start(f32[2,8,256]{2,1,0:T(8,128)} %copy-done.31) | copy-start | bytes 49156
  150.8 7.2 %copy-start.21 = (bf16[1,2,256,256]{2,3,0,1:T(8,128)(2,1)S(1)}, bf16[1,2,256,256]{2,3,0,1:T(8,128)(2,1)}, u32[]{:S(2)}) copy-start(bf16[1,2,256,256]{2,3,0,1:T(8,128)(2,1)} %copy-done.20) | copy-start | bytes 786436
  157.9 7.6 %copy-start.6 = (bf16[1,256,256]{2,1,0:T(8,128)(2,1)S(1)}, bf16[1,256,256]{2,1,0:T(8,128)(2,1)}, u32[]{:S(2)}) copy-start(bf16[1,256,256]{2,1,0:T(8,128)(2,1)} %param.7) | copy-start | bytes 393220
  157.9 7.6 %copy-start.11 = (bf16[1,1,128,256]{3,2,1,0:T(8,128)(2,1)S(1)}, bf16[1,1,128,256]{3,2,1,0:T(8,128)(2,1)}, u32[]{:S(2)}) copy-start(bf16[1,1,128,256]{3,2,1,0:T(8,128)(2,1)} %copy-done.10) | copy-start | bytes 196612
  158.0 7.6 %copy-start.13 = (bf16[1,128,256]{2,1,0:T(8,128)(2,1)S(1)}, bf16[1,128,256]{2,1,0:T(8,128)(2,1)}, u32[]{:S(2)}) copy-start(bf16[1,128,256]{2,1,0:T(8,128)(2,1)} %copy-done.12) | copy-start | bytes 196612
  158.0 7.6 %copy-start.26 = (f32[2,256]{1,0:T(2,128)S(1)}, f32[2,256]{1,0:T(2,128)}, u32[]{:S(2)}) copy-start(f32[2,256]{1,0:T(2,128)} %copy-done.25) | copy-start | bytes 6148
  158.0 7.6 %copy-start.28 = (f32[2,256]{1,0:T(2,128)S(1)}, f32[2,256]{1,0:T(2,128)}, u32[]{:S(2)}) copy-start(f32[2,256]{1,0:T(2,128)} %copy-done.27) | copy-start | bytes 6148
  158.0 7.6 %copy-start.30 = (f32[1,256]{1,0:T(1,128)S(1)}, f32[1,256]{1,0:T(1,128)}, u32[]{:S(2)}) copy-start(f32[1,256]{1,0:T(1,128)} %copy-done.29) | copy-start | bytes 3076
  168.2 80.4 %collective-permute-start.1 = (bf16[1,128,256]{2,1,0:T(8,128)(2,1)S(1)}, bf16[1,128,256]{2,1,0:T(8,128)(2,1)S(1)}, u32[]{:S(2)}, u32[]{:S(2)}) collective-permute-start(bf16[1,128,256]{2,1,0:T(8,128)(2,1)S(1)} %fusion.141), channel_id=1, source_target_pairs={{0,1},{1,2},{2,3},{3,4},{4,5},{5,6},{6,7},{7,8},{8,9},{9,10},{10,1... | collective-permute-start | bytes 196616 | tf_op jit(solution)/shard_map/ppermute | solution.py:16
  (21 other events, 69.1 us)
Sparse Core Ops, SparseCore 0:
  167.9 254.6 all-reduce.3
where the time goes:
time: 435 us; the launch traced here: 433 us
  waiting for transfers between devices  201 us (46%)
  blocking collectives  77.3 us (18%)
  matrix products  75.4 us (17%)
  starting transfers between devices  34.2 us (8%)
  local copies, waits for them, and re-layouts  22.4 us (5%)
  between operations  14.6 us (3%)
  other arithmetic  8.15 us (2%)
    psum x1, waiting for transfers between devices, on_device(): lax.psum((grad_intra, grad_inter, gain_intra, gain_inter), ('dp', 'seq'))  173 us
    psum x1, blocking collectives, on_device(): lax.psum((grad_intra, grad_inter, gain_intra, gain_inter), ('dp', 'seq'))  77.3 us
    dot_general x31, matrix products, product(): return jnp.einsum(form, left, right, preferred_element_type=jnp.float32)  64.5 us
    all_to_all x1, starting transfers between devices, on_device(): lax.all_to_all(inner, 'seq', split_axis=1, concat_axis=3, tiled=True)  19.6 us
    all_to_all x1, waiting for transfers between devices, on_device(): lax.all_to_all(grad_inner, 'seq', split_axis=2, concat_axis=1, tiled=True)  13.8 us
    all_to_all x1, waiting for transfers between devices, on_device(): lax.all_to_all(inner, 'seq', split_axis=1, concat_axis=3, tiled=True)  12.8 us
    sub x3, matrix products, layer_forward(): attend = jax.nn.softmax(scores, axis=-1)  10.9 us
  transfers between devices with their start and end apart: 5, of which 4 were waited for; matrix products, arithmetic and copies ran while one was open for 1% of the time, Pallas kernels for 0%

commit v1 on v0

v1 whole, which is shorter than its diff:
```python
import functools

import jax
import jax.numpy as jnp
from jax import lax
from jax.experimental import pallas as pl
from jax.experimental.pallas import tpu as pltpu
from jax.sharding import PartitionSpec as P

MESH = pl.DeviceIdType.MESH
bf16, f32 = jnp.bfloat16, jnp.float32

H = 8
D = 32
N = 256
R = 256
NR = 8
NG = 16
EPS = 1e-05
C = D**-0.5
LOG2E = 1.4426950408889634


def mm(a, b):
    return jnp.dot(a, b, preferred_element_type=f32)


def head_mask(h):
    lane = lax.broadcasted_iota(jnp.int32, (1, N), 1)
    return jnp.where((lane >= D * h) & (lane < D * (h + 1)), 1.0, 0.0).astype(bf16)


def forward(x, w, gain, s, i, want_out):
    cen = x - jnp.mean(x, -1, keepdims=True)
    inv = lax.rsqrt(jnp.mean(cen * cen, -1, keepdims=True) + EPS)
    normed = cen * inv
    s["normed"][i] = normed
    s["inv"][i] = inv
    hidden = (normed * gain).astype(bf16)
    s["hiddenT"][:, i * R : (i + 1) * R] = hidden.T
    q = mm(hidden, w[0])
    s["q"][i] = q.astype(bf16)
    s["qT"][i] = (q * (C * LOG2E)).astype(bf16).T
    k = mm(hidden, w[1]).astype(bf16)
    s["k"][i] = k
    s["kT"][i] = k.T
    v = mm(hidden, w[2]).astype(bf16)
    s["v"][i] = v
    s["vT"][i] = v.T
    for h in range(H):
        rows = slice(D * h, D * (h + 1))
        scores = mm(s["k"][i] * head_mask(h), s["qT"][i])
        p = jnp.exp2(scores - jnp.max(scores, 0, keepdims=True))
        a = (p * (1.0 / jnp.sum(p, 0, keepdims=True))).astype(bf16)
        s["A"][i, :, h * R : (h + 1) * R] = a
        s["combT"][i, rows, :] = mm(s["vT"][i, rows, :], a)
    if want_out:
        return x + mm(s["combT"][i].astype(bf16).T, w[3])
    return None


def backward(g, w3T, wT, gain, s, i):
    gc = mm(g, w3T[...]).astype(bf16)
    s["gcT"][...] = gc.T
    for h in range(H):
        mask = head_mask(h)
        rows = slice(D * h, D * (h + 1))
        cols = slice(h * R, (h + 1) * R)
        s["gcs"][cols, :] = gc * mask
        s["qs"][cols, :] = s["q"][i] * mask
        ga = mm(s["v"][i] * mask, s["gcT"][...])
        drow = jnp.sum(s["gcT"][rows, :].astype(f32) * s["combT"][i, rows, :], 0, keepdims=True)
        d = (s["A"][i, :, cols].astype(f32) * (ga - drow)).astype(bf16)
        s["Dm"][:, cols] = d
        s["gqT"][rows, :] = (mm(s["kT"][i, rows, :], d) * C).astype(bf16)
    gv = mm(s["A"][i], s["gcs"][...]).astype(bf16)
    gk = (mm(s["Dm"][...], s["qs"][...]) * C).astype(bf16)
    gqkv = jnp.concatenate([s["gqT"][...].T, gk, gv], axis=1)
    s["gqkv"][i * R : (i + 1) * R, :] = gqkv
    gh = mm(gqkv, wT[...])
    normed = s["normed"][i]
    ggain = jnp.sum(gh * normed, 0, keepdims=True)
    t = gh * gain
    dx = g.astype(f32) + s["inv"][i] * (
        t - jnp.mean(t, -1, keepdims=True) - normed * jnp.mean(t * normed, -1, keepdims=True)
    )
    return dx, ggain


def saved_scratch():
    def square(kind):
        return pltpu.VMEM((2, R, N), kind)

    return dict(
        normed=square(f32),
        inv=pltpu.VMEM((2, R, 1), f32),
        hiddenT=pltpu.VMEM((N, 2 * R), bf16),
        q=square(bf16),
        qT=square(bf16),
        k=square(bf16),
        kT=square(bf16),
        v=square(bf16),
        vT=square(bf16),
        A=pltpu.VMEM((2, R, H * R), bf16),
        combT=square(f32),
        gqkv=pltpu.VMEM((2 * R, 3 * N), bf16),
    )


def shared_scratch():
    return dict(
        gcT=pltpu.VMEM((N, R), bf16),
        gcs=pltpu.VMEM((H * R, N), bf16),
        qs=pltpu.VMEM((H * R, N), bf16),
        Dm=pltpu.VMEM((R, H * R), bf16),
        gqT=pltpu.VMEM((N, R), bf16),
    )


def weight_scratch():
    return dict(wT=pltpu.VMEM((3 * N, N), bf16), w3T=pltpu.VMEM((N, N), bf16))


def comm_scratch():
    dma = pltpu.SemaphoreType.DMA
    block = pltpu.VMEM((2, NG, 16, N), bf16)
    near = pltpu.VMEM((NR, 2, 2, 16, N), bf16)
    bufs = dict(
        halo=pltpu.VMEM((R // 2, N), bf16),
        tail=pltpu.VMEM((R // 2, N), bf16),
        tail_in=pltpu.VMEM((R // 2, N), bf16),
        a_out=block,
        a_in=block,
        b_out=pltpu.VMEM((2, NR, 2, 16, N), bf16),
        b_in=near,
        rb_out=pltpu.VMEM((2, NR, 2, 16, N), bf16),
        rb_in=near,
        ra_out=block,
        ra_in=block,
        s1_out=pltpu.VMEM((2, NR, 144, N), bf16),
        s1_in=pltpu.VMEM((2, NR, 144, N), bf16),
        s2_out=pltpu.VMEM((2, NG, 32, 128), bf16),
        s2_in=pltpu.VMEM((2, NG, 32, 128), bf16),
        s3_out=pltpu.VMEM((2, 32, 128), f32),
        s3_in=pltpu.VMEM((2, 32, 128), f32),
        g2=pltpu.VMEM((2, NG, 16, 128), bf16),
        g1=pltpu.VMEM((2, NR, 128, N), bf16),
    )
    sems = {}
    for name, shape in dict(
        halo=(1, 1),
        tail=(1, 1),
        a=(2, NG),
        b=(2, NR),
        rb=(2, NR),
        ra=(2, NG),
        s1=(2, NR),
        s2=(2, NG),
        s3=(2, 1),
        g2=(2, NG),
        g1=(2, NR),
    ).items():
        sems[name + "_send"] = dma(shape)
        sems[name + "_recv"] = dma(shape)
    return bufs, sems


def loop(lo, hi, f):
    def step(d, carry):
        f(d)
        return carry

    lax.fori_loop(lo, hi, step, 0)


def kernel(n_seq, frames, upstream, w1, w2, gains, gf, gw1, gw2, gg, s1, s2, shared, wt1, wt2, bufs, sems):
    s1, s2 = dict(s1, **shared), dict(s2, **shared)
    me, dp = lax.axis_index("seq"), lax.axis_index("dp")
    g, r = lax.div(me, NR), lax.rem(me, NR)
    right, left = lax.rem(me + 1, n_seq), lax.rem(me + n_seq - 1, n_seq)

    def far(gg_):
        return {"seq": gg_ * NR + r}

    def near(rr):
        return {"seq": g * NR + rr}

    def ahead(d, n, mine):
        return lax.rem(mine + d, n)

    def behind(d, n, mine):
        return lax.rem(mine + n - d, n)

    def copy(name, c, d, src, dst, to):
        return pltpu.make_async_remote_copy(
            src_ref=src,
            dst_ref=dst,
            send_sem=sems[name + "_send"].at[c, d],
            recv_sem=sems[name + "_recv"].at[c, d],
            device_id=to,
            device_id_type=MESH,
        )

    class Exchange:
        def __init__(self, name, c, n, mine, address, src, dst):
            self.n = n

            def out(d):
                peer = ahead(d, n, mine)
                return copy(name, c, d, src(peer), dst(mine), address(peer))

            def came(d):
                peer = behind(d, n, mine)
                return copy(name, c, d, src(peer), dst(peer), address(peer))

            self.out, self.came = out, came

        def start(self):
            loop(1, self.n, lambda d: self.out(d).start())

        def wait_recv(self):
            loop(1, self.n, lambda d: self.came(d).wait_recv())

        def wait_send(self):
            loop(1, self.n, lambda d: self.out(d).wait_send())

    def far_exchange(name, c, src, dst):
        return Exchange(name, c, NG, g, far, src, dst)

    def near_exchange(name, c, src, dst):
        return Exchange(name, c, NR, r, near, src, dst)

    b = bufs
    ex_a = [far_exchange("a", c, lambda p, c=c: b["a_out"].at[c, p], lambda p, c=c: b["a_in"].at[c, p]) for c in range(2)]
    ex_b = [near_exchange("b", c, lambda p, c=c: b["b_out"].at[c, p], lambda p, c=c: b["b_in"].at[p, c]) for c in range(2)]
    ex_rb = [near_exchange("rb", c, lambda p, c=c: b["rb_out"].at[c, p], lambda p, c=c: b["rb_in"].at[p, c]) for c in range(2)]
    ex_ra = [far_exchange("ra", c, lambda p, c=c: b["ra_out"].at[c, p], lambda p, c=c: b["ra_in"].at[c, p]) for c in range(2)]
    ex_s1 = [near_exchange("s1", c, lambda p, c=c: b["s1_out"].at[c, p], lambda p, c=c: b["s1_in"].at[c, p]) for c in range(2)]
    ex_s2 = [far_exchange("s2", c, lambda p, c=c: b["s2_out"].at[c, p], lambda p, c=c: b["s2_in"].at[c, p]) for c in range(2)]
    ex_g2 = [far_exchange("g2", c, lambda p, c=c: b["g2"].at[c, g], lambda p, c=c: b["g2"].at[c, p]) for c in range(2)]
    ex_g1 = [near_exchange("g1", c, lambda p, c=c: b["g1"].at[c, r], lambda p, c=c: b["g1"].at[c, p]) for c in range(2)]
    ex_s3 = [copy("s3", c, 0, b["s3_out"].at[c], b["s3_in"].at[c], {"dp": 1 - dp}) for c in range(2)]

    barrier = pltpu.get_barrier_semaphore()

    def greet(device):
        pl.semaphore_signal(barrier, inc=1, device_id=device, device_id_type=MESH)

    loop(1, NG, lambda d: greet(far(ahead(d, NG, g))))
    loop(1, NR, lambda d: greet(near(ahead(d, NR, r))))
    greet({"seq": right})
    greet({"seq": left})
    greet({"dp": 1 - dp})

    row = lax.broadcasted_iota(jnp.int32, (R, R), 0)
    col = lax.broadcasted_iota(jnp.int32, (R, R), 1)
    swap = jnp.where((row % 16) * 16 + row // 16 == col, 1.0, 0.0).astype(bf16)

    def swapped(x):
        return mm(swap, x).astype(bf16)

    for w, wt in ((w1, wt1), (w2, wt2)):
        for j in range(3):
            wt["wT"][j * N : (j + 1) * N, :] = w[j].T
        wt["w3T"][...] = w[3].T
    g1, g2 = gains[0:1], gains[1:2]

    pl.semaphore_wait(barrier, NG - 1 + NR - 1 + 3)
    halo = copy("halo", 0, 0, frames.at[0, 0 : R // 2], b["halo"], {"seq": left})
    halo.start()

    def spread(c, out):
        out = out.astype(bf16).reshape(NG, 16, N)
        b["a_out"][c] = out
        ex_a[c].start()
        b["a_in"][c, g] = b["a_out"][c, g]

    def regroup(c):
        ex_a[c].wait_recv()
        b["b_out"][c] = swapped(b["a_in"][c].reshape(R, N)).reshape(NR, 2, 16, N)
        ex_b[c].start()
        b["b_in"][r, c] = b["b_out"][c, r]

    own = frames[0].astype(f32)
    spread(0, forward(own, w1, g1, s1, 0, True))
    halo.wait_recv()
    following = jnp.where(me < n_seq - 1, b["halo"][...].astype(f32), 0.0)
    out1 = forward(jnp.concatenate([own[R // 2 :], following], 0), w1, g1, s1, 1, True)
    regroup(0)
    spread(1, out1)
    upper = [swapped(upstream[0, i]) for i in range(2)]
    regroup(1)
    for c in range(2):
        ex_b[c].wait_recv()

    gain2 = jnp.zeros((1, N), f32)
    g3 = jnp.zeros((N, N), f32)
    for i in range(2):
        forward(b["b_in"][:, :, i].reshape(R, N).astype(f32), w2, g2, s2, i, False)
        dx, gain = backward(upper[i], wt2["w3T"], wt2["wT"], g2, s2, i)
        gain2 += gain
        b["rb_out"][i] = dx.astype(bf16).reshape(NR, 2, 16, N)
        ex_rb[i].start()
        b["rb_in"][r, i] = b["rb_out"][i, r]
        g3 += mm(s2["combT"][i].astype(bf16), upper[i])

    row16 = lax.broadcasted_iota(jnp.int32, (16, 1), 0)

    def two_rows(x):
        high = x.astype(bf16).astype(f32)
        return jnp.where(row16 == 0, high, jnp.where(row16 == 1, x - high, 0.0))

    def sum_start(a, proj, out, gain):
        for j in range(4):
            m = out if j == 3 else proj[:, j * N : (j + 1) * N]
            b["s1_out"][a, 2 * j : 2 * j + 2, 0:128, :] = m.astype(bf16).reshape(2, 128, N)
        rows = two_rows(gain).astype(bf16)
        for p in range(NR):
            b["s1_out"][a, p, 128:144, :] = rows
        ex_s1[a].start()
        b["s1_in"][a, r] = b["s1_out"][a, r]

    def sum_second(a):
        ex_s1[a].wait_recv()
        total = b["s1_in"][a, 0].astype(f32)
        for p in range(1, NR):
            total += b["s1_in"][a, p].astype(f32)
        gain = total[128:129] + total[129:130]
        rows = two_rows(gain)
        rows = rows[:, 0:128] + jnp.where(
            row16 == 2, rows[0:1, 128:256], jnp.where(row16 == 3, rows[1:2, 128:256], 0.0)
        )
        rows = rows.astype(bf16)
        for p in range(NG):
            i, j = p // 2, p % 2
            b["s2_out"][a, p, 0:16] = total[16 * i : 16 * i + 16, 128 * j : 128 * j + 128].astype(bf16)
            b["s2_out"][a, p, 16:32] = rows
        ex_s2[a].start()
        b["s2_in"][a, g] = b["s2_out"][a, g]

    def sum_third(a):
        ex_s2[a].wait_recv()
        total = b["s2_in"][a, 0].astype(f32)
        for p in range(1, NG):
            total += b["s2_in"][a, p].astype(f32)
        b["s3_out"][a] = total
        ex_s3[a].start()

    def sum_fourth(a):
        ex_s3[a].wait_recv()
        total = b["s3_out"][a] + b["s3_in"][a]
        b["g2"][a, g] = total[0:16].astype(bf16)
        ex_g2[a].start()
        gg[a : a + 1, 0:128] = total[16:17] + total[17:18]
        gg[a : a + 1, 128:256] = total[18:19] + total[19:20]

    def sum_fifth(a):
        ex_g2[a].wait_recv()
        for p in range(NG):
            i, j = p // 2, p % 2
            b["g1"][a, r, 16 * i : 16 * i + 16, 128 * j : 128 * j + 128] = b["g2"][a, p]
        ex_g1[a].start()

    def sum_finish(a, gw):
        ex_g1[a].wait_recv()
        for p in range(NR):
            gw[p // 2, 128 * (p % 2) : 128 * (p % 2) + 128, :] = b["g1"][a, p].astype(f32)

    for c in range(2):
        ex_rb[c].wait_recv()
    for c in (1, 0):
        back = b["rb_in"][:, :, c].reshape(R, N)
        b["ra_out"][c] = swapped(back).reshape(NG, 16, N)
        ex_ra[c].start()
        b["ra_in"][c, g] = b["ra_out"][c, g]
    sum_start(1, mm(s2["hiddenT"][...], s2["gqkv"][...]), g3, gain2)

    ex_ra[1].wait_recv()
    top1 = b["ra_in"][1].reshape(R, N)
    dx1, gain1 = backward(top1, wt1["w3T"], wt1["wT"], g1, s1, 1)
    b["tail"][...] = dx1[R // 2 :].astype(bf16)
    tail = copy("tail", 0, 0, b["tail"], b["tail_in"], {"seq": right})
    tail.start()
    sum_second(1)
    ex_ra[0].wait_recv()
    top0 = b["ra_in"][0].reshape(R, N)
    g3 = mm(s1["combT"][0].astype(bf16), top0) + mm(s1["combT"][1].astype(bf16), top1)
    dx0, gain0 = backward(top0, wt1["w3T"], wt1["wT"], g1, s1, 0)
    sum_start(0, mm(s1["hiddenT"][...], s1["gqkv"][...]), g3, gain0 + gain1)
    tail.wait_recv()
    carried = jnp.where(me > 0, b["tail_in"][...].astype(f32), 0.0)
    gf[0, 0 : R // 2] = (dx0[0 : R // 2] + carried).astype(bf16)
    gf[0, R // 2 :] = (dx0[R // 2 :] + dx1[0 : R // 2]).astype(bf16)
    sum_third(1)
    sum_second(0)
    sum_fourth(1)
    sum_third(0)
    sum_fifth(1)
    sum_fourth(0)
    sum_fifth(0)
    sum_finish(1, gw2)
    sum_finish(0, gw1)

    halo.wait_send()
    tail.wait_send()
    for group in (ex_a, ex_b, ex_rb, ex_ra, ex_s1, ex_s2, ex_s3, ex_g2, ex_g1):
        for c in range(2):
            group[c].wait_send()


def on_device(n_seq, frames, upstream, w1, w2, gains):
    vmem = pl.BlockSpec(memory_space=pltpu.VMEM)
    bufs, sems = comm_scratch()
    return pl.pallas_call(
        functools.partial(kernel, n_seq),
        in_specs=[vmem] * 5,
        out_specs=[vmem] * 4,
        out_shape=[
            jax.ShapeDtypeStruct(frames.shape, bf16),
            jax.ShapeDtypeStruct(w1.shape, f32),
            jax.ShapeDtypeStruct(w2.shape, f32),
            jax.ShapeDtypeStruct(gains.shape, f32),
        ],
        scratch_shapes=[
            saved_scratch(),
            saved_scratch(),
            shared_scratch(),
            weight_scratch(),
            weight_scratch(),
            bufs,
            sems,
        ],
        compiler_params=pltpu.CompilerParams(
            collective_id=0, has_side_effects=True, vmem_limit_bytes=56 * 2**20
        ),
        name="block_backward",
    )(frames, upstream, w1, w2, gains)


def solution(mesh):
    placed = (P("dp", "seq", None), P("dp", "seq", None, None), P(), P(), P())
    return jax.shard_map(
        functools.partial(on_device, mesh.shape["seq"]),
        mesh=mesh,
        in_specs=placed,
        out_specs=(P("dp", "seq", None), P(), P(), P()),
        check_vma=False,
    )
```

time: 435 us -> 107 us (0.25)
  waiting for transfers between devices: 201 us -> 0 us
  Pallas kernels: 0 us -> 100 us
  blocking collectives: 77.3 us -> 0 us
  matrix products: 75.4 us -> 0 us
  starting transfers between devices: 34.2 us -> 0 us
  local copies, waits for them, and re-layouts: 22.4 us -> 5.5 us
  between operations: 14.6 us -> 0.64 us
  other arithmetic: 8.15 us -> 0 us
    psum x1 -> x0, waiting for transfers between devices: 173 us -> none  [on_device(): lax.psum((grad_intra, grad_inter, gain_intra, gain_inter), ('dp', 'seq'))]
    pallas_call x0 -> x1, Pallas kernels: none -> 100 us  [on_device(): pl.pallas_call(functools.partial(kernel, n_seq), in_specs=[vmem] * 5, out...]
    psum x1 -> x0, blocking collectives: 77.3 us -> none  [on_device(): lax.psum((grad_intra, grad_inter, gain_intra, gain_inter), ('dp', 'seq'))]
    dot_general x31 -> x0, matrix products: 64.5 us -> none  [product(): return jnp.einsum(form, left, right, preferred_element_type=jnp.float32)]
    all_to_all x2 -> x0, waiting for transfers between devices: 26.6 us -> none  [the longest x1 13.8 us: on_device(): lax.all_to_all(grad_inner, 'seq', split_axis=2, concat_axis=1, tiled=True)]
    all_to_all x2 -> x0, starting transfers between devices: 26.6 us -> none  [the longest x1 19.6 us: on_device(): lax.all_to_all(inner, 'seq', split_axis=1, concat_axis=3, tiled=True)]
    sub x3 -> x0, matrix products: 10.9 us -> none  [layer_forward(): attend = jax.nn.softmax(scores, axis=-1)]
    ppermute x2 -> x0, starting transfers between devices: 7.63 us -> none  [shifted(): return lax.ppermute(block, axis, route)]
  transfers between devices with their start and end apart: 5 -> 0, of which waited for: 4 -> 0; matrix products, arithmetic and copies ran while one was open for 1% -> 0% of each run, Pallas kernels for 0% -> 0%
where the time goes in v1:
time: 107 us
  Pallas kernels  100 us (93%)
  local copies, waits for them, and re-layouts  5.5 us (5%)
    pallas_call x1, Pallas kernels, on_device(): pl.pallas_call(functools.partial(kernel, n_seq), in_specs=[vmem] * 5, out...  100 us
    unnamed x8, local copies, waits for them, and re-layouts  5.5 us

profile of v1, /device:TPU:1, one launch (start us, length us, event | category | flops | bytes accessed | tf_op | source)
XLA Modules:
  0.0 106.5 jit_solution(1091651105390009278)
XLA Ops:
  0.6 100.4 %block_backward.1 = (bf16[1,256,256]{2,1,0:T(8,128)(2,1)}, f32[4,256,256]{2,1,0:T(8,128)}, f32[4,256,256]{2,1,0:T(8,128)}, f32[2,256]{1,0:T(2,128)}) custom-call(bf16[1,256,256]{2,1,0:T(8,128)(2,1)} %frames.1, bf16[1,2,256,256]{3,2,1,0:T(8,128)(2,1)} %upstream.1, bf16[4,256,256]{2,1,0:T(8,128)(2,1)} %w1.1, bf16[4,256,256]{2,1,0:T(8,128)(2,1)} %w2.1, ...), custom_call_target="tpu_custom_call" | custom-call | tf_op jit(solution)/shard_map/block_backward/pallas_call | solution.py:414
  101.0 1.6 %copy.13 = bf16[1,256,256]{2,1,0:T(8,128)(2,1)} copy(bf16[1,256,256]{2,1,0:T(8,128)(2,1)} %get-tuple-element.8) | data formatting | bytes 262144
  102.6 0.0 copy-start
  102.6 2.4 %copy.14 = f32[4,256,256]{2,1,0:T(8,128)} copy(f32[4,256,256]{2,1,0:T(8,128)} %get-tuple-element.9) | data formatting | bytes 2097152
  105.0 0.0 copy-done
  105.0 0.0 copy-start.1
  105.0 1.0 copy.15
  105.9 0.0 copy-done.1
  105.9 0.6 copy.16
Async XLA Ops:
  102.6 2.4 %copy-start = (f32[4,256,256]{2,1,0:T(8,128)S(1)}, f32[4,256,256]{2,1,0:T(8,128)}, u32[]{:S(2)}) copy-start(f32[4,256,256]{2,1,0:T(8,128)} %get-tuple-element.10) | copy-start | bytes 3145732
  105.0 1.0 copy-start.1

commit v2 on v1

v2 whole, which is shorter than its diff:
```python
import functools

import jax
import jax.numpy as jnp
from jax import lax
from jax.experimental import pallas as pl
from jax.experimental.pallas import tpu as pltpu
from jax.sharding import PartitionSpec as P

MESH = pl.DeviceIdType.MESH
bf16, f32 = jnp.bfloat16, jnp.float32

H = 8
D = 32
N = 256
R = 256
NR = 8
NG = 16
X, ZH, Y, CORE = 4, 4, 4, 2
DP = 2
Z = ZH * DP
EPS = 1e-05
C = D**-0.5
LOG2E = 1.4426950408889634


def mm(a, b):
    return jnp.dot(a, b, preferred_element_type=f32)


def head_mask(h):
    lane = lax.broadcasted_iota(jnp.int32, (1, N), 1)
    return jnp.where((lane >= D * h) & (lane < D * (h + 1)), 1.0, 0.0).astype(bf16)


def forward(x, w, gain, s, i, want_out):
    cen = x - jnp.mean(x, -1, keepdims=True)
    inv = lax.rsqrt(jnp.mean(cen * cen, -1, keepdims=True) + EPS)
    normed = cen * inv
    s["normed"][i] = normed
    s["inv"][i] = inv
    hidden = (normed * gain).astype(bf16)
    s["hiddenT"][:, i * R : (i + 1) * R] = hidden.T
    q = mm(hidden, w[0])
    s["q"][i] = q.astype(bf16)
    s["qT"][i] = (q * (C * LOG2E)).astype(bf16).T
    k = mm(hidden, w[1]).astype(bf16)
    s["k"][i] = k
    s["kT"][i] = k.T
    v = mm(hidden, w[2]).astype(bf16)
    s["v"][i] = v
    s["vT"][i] = v.T
    for h in range(H):
        rows = slice(D * h, D * (h + 1))
        scores = mm(s["k"][i] * head_mask(h), s["qT"][i])
        p = jnp.exp2(scores - jnp.max(scores, 0, keepdims=True))
        a = (p * (1.0 / jnp.sum(p, 0, keepdims=True))).astype(bf16)
        s["A"][i, :, h * R : (h + 1) * R] = a
        s["combT"][i, rows, :] = mm(s["vT"][i, rows, :], a)
    if want_out:
        return x + mm(s["combT"][i].astype(bf16).T, w[3])
    return None


def spread_heads(x, out):
    for h in range(H):
        out[h * R : (h + 1) * R, :] = x * head_mask(h)


def back_start(g, w3T, s, i):
    gc = mm(g, w3T[...]).astype(bf16)
    s["gcT"][i] = gc.T
    spread_heads(gc, s["gcs"].at[i])


def back_heads(s, i):
    for h in range(H):
        rows = slice(D * h, D * (h + 1))
        cols = slice(h * R, (h + 1) * R)
        ga = mm(s["v"][i] * head_mask(h), s["gcT"][i])
        drow = jnp.sum(s["gcT"][i, rows, :].astype(f32) * s["combT"][i, rows, :], 0, keepdims=True)
        d = (s["A"][i, :, cols].astype(f32) * (ga - drow)).astype(bf16)
        s["Dm"][:, cols] = d
        s["gqT"][rows, :] = (mm(s["kT"][i, rows, :], d) * C).astype(bf16)
    mine = slice(i * R, (i + 1) * R)
    s["gqkv"][mine, 2 * N : 3 * N] = mm(s["A"][i], s["gcs"][i]).astype(bf16)
    s["gqkv"][mine, N : 2 * N] = (mm(s["Dm"][...], s["qs"][i]) * C).astype(bf16)
    s["gqkv"][mine, 0:N] = s["gqT"][...].T


def back_input(g, wT, gain, s, i):
    gh = mm(s["gqkv"][i * R : (i + 1) * R, :], wT[...])
    normed = s["normed"][i]
    t = gh * gain
    return g.astype(f32) + s["inv"][i] * (
        t - jnp.mean(t, -1, keepdims=True) - normed * jnp.mean(t * normed, -1, keepdims=True)
    )


def saved_scratch():
    def square(kind):
        return pltpu.VMEM((2, R, N), kind)

    def heads():
        return pltpu.VMEM((2, H * R, N), bf16)

    return dict(
        normed=square(f32),
        inv=pltpu.VMEM((2, R, 1), f32),
        hiddenT=pltpu.VMEM((N, 2 * R), bf16),
        q=square(bf16),
        qT=square(bf16),
        k=square(bf16),
        kT=square(bf16),
        v=square(bf16),
        vT=square(bf16),
        A=pltpu.VMEM((2, R, H * R), bf16),
        combT=square(f32),
        gqkv=pltpu.VMEM((2 * R, 3 * N), bf16),
        gcT=square(bf16),
        gcs=heads(),
        qs=heads(),
    )


def shared_scratch():
    return dict(Dm=pltpu.VMEM((R, H * R), bf16), gqT=pltpu.VMEM((N, R), bf16))


def weight_scratch():
    return dict(w=pltpu.VMEM((4, N, N), bf16), wT=pltpu.VMEM((3 * N, N), bf16), w3T=pltpu.VMEM((N, N), bf16))


SUMS = {"inter": 4, "out": 1, "proj": 3}


def comm_scratch():
    dma = pltpu.SemaphoreType.DMA
    half = pltpu.VMEM((R // 2, N), bf16)
    far = pltpu.VMEM((2, NG, 16, N), bf16)
    near = pltpu.VMEM((2, NR, 2, 16, N), bf16)
    bufs = dict(
        frames=pltpu.VMEM((R, N), bf16),
        upstream=pltpu.VMEM((2, R, N), bf16),
        gains=pltpu.VMEM((2, N), f32),
        upper=pltpu.VMEM((2, R, N), bf16),
        top=pltpu.VMEM((2, R, N), bf16),
        swap=pltpu.VMEM((R, R), bf16),
        turn=pltpu.VMEM((R, R), bf16),
        gather=pltpu.VMEM((2, R, 2 * R), bf16),
        halo=half,
        tail=half,
        tail_in=half,
        a_out=far,
        a_in=far,
        b_out=near,
        b_in=near,
        rb_out=near,
        rb_in=near,
        ra_out=far,
        ra_in=far,
    )
    count = dict(inputs=5, halo=1, tail=1, a=2 * NG, b=2 * NR, rb=2 * NR, ra=2 * NG)
    for name, m in SUMS.items():
        bufs[name + "_pair"] = pltpu.VMEM((CORE, NG, m, 16, 128), bf16)
        bufs[name + "_pair_in"] = pltpu.VMEM((NG, m, 16, 128), bf16)
        bufs[name + "_xy"] = pltpu.VMEM((NG, m, 16, 128), bf16)
        bufs[name + "_xy_in"] = pltpu.VMEM((NG, m, 16, 128), bf16)
        bufs[name + "_z"] = pltpu.VMEM((Z, m, 16, 128), bf16)
        bufs[name + "_all"] = pltpu.VMEM((CORE, NG, m, 16, 128), bf16)
        for stage, n in dict(pair=1, xy=NG, z=Z, share=NG, last=1).items():
            count[name + "_" + stage] = n
    sems = {}
    for name, n in count.items():
        sems[name + "_send"] = dma((n,))
        sems[name + "_recv"] = dma((n,))
    return bufs, sems


def loop(lo, hi, f):
    def step(d, carry):
        f(d)
        return carry

    lax.fori_loop(lo, hi, step, 0)


def digits(index, *sizes):
    found = []
    for n in reversed(sizes):
        found.append(jnp.bitwise_and(index, n - 1))
        index = jnp.right_shift(index, n.bit_length() - 1)
    return found[::-1]


def selection(rows, cols, source):
    row = lax.broadcasted_iota(jnp.int32, (rows, cols), 0)
    col = lax.broadcasted_iota(jnp.int32, (rows, cols), 1)
    return jnp.where(source(row) == col, 1.0, 0.0).astype(bf16)


def kernel(n_seq, frames_hbm, upstream_hbm, w1_hbm, w2_hbm, gains_hbm, gf, gw1, gw2, gg, s1, s2, shared, wt1, wt2, b, sems):
    s1, s2 = dict(s1, **shared), dict(s2, **shared)
    me, dp = lax.axis_index("seq"), lax.axis_index("dp")
    g, r = lax.div(me, NR), lax.rem(me, NR)
    x, zh = lax.div(g, ZH), lax.rem(g, ZH)
    y, core = lax.div(r, CORE), lax.rem(r, CORE)
    xy, z = x * Y + y, zh * DP + dp
    right, left = lax.rem(me + 1, n_seq), lax.rem(me + n_seq - 1, n_seq)

    def at_far(p):
        return {"seq": p * NR + r}

    def at_near(p):
        return {"seq": g * NR + p}

    def at_xy(p):
        return {"seq": ((lax.div(p, Y) * ZH + zh) * Y + lax.rem(p, Y)) * CORE + core}

    def at_z(p):
        return {"seq": ((x * ZH + lax.div(p, DP)) * Y + y) * CORE + core, "dp": lax.rem(p, DP)}

    other_core = {"seq": me + 1 - 2 * core}

    inputs = [
        pltpu.make_async_copy(src, dst, sems["inputs_send"].at[i])
        for i, (src, dst) in enumerate(
            (
                (frames_hbm.at[0], b["frames"]),
                (w1_hbm, wt1["w"]),
                (gains_hbm, b["gains"]),
                (upstream_hbm.at[0], b["upstream"]),
                (w2_hbm, wt2["w"]),
            )
        )
    ]
    for c in inputs:
        c.start()

    barrier = pltpu.get_barrier_semaphore()

    def greet(device):
        pl.semaphore_signal(barrier, inc=1, device_id=device, device_id_type=MESH)

    loop(1, NG, lambda d: greet(at_far(lax.rem(g + d, NG))))
    loop(0, ZH, lambda d: greet(at_z(lax.rem(zh + d, ZH) * DP + 1 - dp)))
    loop(
        0,
        (X - 1) * (Y - 1),
        lambda d: greet(
            at_xy(lax.rem(x + 1 + lax.div(d, Y - 1), X) * Y + lax.rem(y + 1 + lax.rem(d, Y - 1), Y))
        ),
    )
    loop(1, NR, lambda d: greet(at_near(lax.rem(r + d, NR))))
    greet({"seq": right})
    greet({"seq": left})
    greetings = NG - 1 + ZH + (X - 1) * (Y - 1) + NR - 1 + 2

    def copy(name, d, src, dst, to):
        return pltpu.make_async_remote_copy(
            src_ref=src,
            dst_ref=dst,
            send_sem=sems[name + "_send"].at[d],
            recv_sem=sems[name + "_recv"].at[d],
            device_id=to,
            device_id_type=MESH,
        )

    class Exchange:
        started = []

        def __init__(self, name, n, mine, address, src, dst, first=0):
            self.n = n

            def out(d):
                peer = lax.rem(mine + d, n)
                return copy(name, first + d, src(peer), dst(mine), address(peer))

            def came(d):
                peer = lax.rem(mine + n - d, n)
                return copy(name, first + d, src(peer), dst(peer), address(peer))

            self.out, self.came = out, came

        def start(self):
            loop(1, self.n, lambda d: self.out(d).start())
            self.started.append(self)

        def wait_recv(self):
            loop(1, self.n, lambda d: self.came(d).wait_recv())

        def wait_send(self):
            loop(1, self.n, lambda d: self.out(d).wait_send())

    def far_exchange(name, i):
        out, into = b[name + "_out"], b[name + "_in"]
        return Exchange(name, NG, g, at_far, lambda p: out.at[i, p], lambda p: into.at[i, p], NG * i)

    def near_exchange(name, i):
        out, into = b[name + "_out"], b[name + "_in"]
        return Exchange(name, NR, r, at_near, lambda p: out.at[i, p], lambda p: into.at[i, p], NR * i)

    ex_a = [far_exchange("a", c) for c in range(2)]
    ex_b = [near_exchange("b", i) for i in range(2)]
    ex_rb = [near_exchange("rb", i) for i in range(2)]
    ex_ra = [far_exchange("ra", i) for i in range(2)]

    class Sum:
        def __init__(self, name):
            self.m = SUMS[name]
            pair, pair_in = b[name + "_pair"], b[name + "_pair_in"]
            every = b[name + "_all"]
            self.pair, self.pair_in, self.every = pair, pair_in, every
            self.xy, self.xy_in, self.z = b[name + "_xy"], b[name + "_xy_in"], b[name + "_z"]
            self.ex_pair = copy(name + "_pair", 0, pair.at[1 - core], pair_in, other_core)
            self.ex_xy = Exchange(
                name + "_xy", NG, xy, at_xy, lambda p: self.xy.at[p], lambda p: self.xy_in.at[p]
            )
            self.ex_z = Exchange(name + "_z", Z, z, at_z, lambda p: self.z.at[z], lambda p: self.z.at[p])
            self.ex_share = Exchange(
                name + "_share", NG, xy, at_xy, lambda p: every.at[core, xy], lambda p: every.at[core, p]
            )
            self.ex_last = copy(name + "_last", 0, every.at[core], every.at[core], other_core)
            self.ex_last_in = copy(name + "_last", 0, every.at[1 - core], every.at[1 - core], other_core)

        def put(self, j, matrix):
            matrix = matrix.astype(bf16)
            for k in range(CORE):
                for p in range(NG):
                    row, lane = k * 128 + p // 2 * 16, p % 2 * 128
                    self.pair[k, p, j] = matrix[row : row + 16, lane : lane + 128]

        def first(self):
            self.ex_pair.start()

        def second(self):
            self.ex_pair.wait_recv()
            total = self.pair[core].astype(f32) + self.pair_in[...].astype(f32)
            self.xy[...] = total.astype(bf16)
            self.ex_xy.start()
            self.xy_in[xy] = self.xy[xy]

        def third(self):
            self.ex_xy.wait_recv()
            total = self.xy_in[0].astype(f32)
            for p in range(1, NG):
                total += self.xy_in[p].astype(f32)
            self.z[z] = total.astype(bf16)
            self.ex_z.start()

        def fourth(self):
            self.ex_z.wait_recv()
            total = self.z[0].astype(f32)
            for p in range(1, Z):
                total += self.z[p].astype(f32)
            self.every[core, xy] = total.astype(bf16)
            self.ex_share.start()

        def fifth(self):
            self.ex_share.wait_recv()
            self.ex_last.start()

        def finish(self, out, first):
            self.ex_last_in.wait_recv()
            for k in range(CORE):
                for p in range(NG):
                    row, lane = k * 128 + p // 2 * 16, p % 2 * 128
                    for j in range(self.m):
                        out[first + j, row : row + 16, lane : lane + 128] = self.every[k, p, j]

        def wait_send(self):
            self.ex_pair.wait_send()
            self.ex_last.wait_send()

    sum_inter, sum_out, sum_proj = Sum("inter"), Sum("out"), Sum("proj")

    def spread(c, out):
        b["a_out"][c] = out.astype(bf16).reshape(NG, 16, N)
        ex_a[c].start()
        b["a_in"][c, g] = b["a_out"][c, g]

    for c in inputs[:3]:
        c.wait()
    g1, g2 = b["gains"][0:1], b["gains"][1:2]
    own = b["frames"][...].astype(f32)
    out0 = forward(own, wt1["w"], g1, s1, 0, True)

    pl.semaphore_wait(barrier, greetings)
    halo = copy("halo", 0, b["frames"].at[0 : R // 2], b["halo"], {"seq": left})
    halo.start()
    spread(0, out0)

    b["swap"][...] = selection(R, R, lambda i: (lambda u, v: v * 16 + u)(*digits(i, 16, 16)))
    for c in inputs[3:]:
        c.wait()
    for i in range(2):
        b["upper"][i] = mm(b["swap"][...], b["upstream"][i]).astype(bf16)

    halo.wait_recv()
    following = jnp.where(me < n_seq - 1, b["halo"][...].astype(f32), 0.0)
    spread(1, forward(jnp.concatenate([own[R // 2 :], following], 0), wt1["w"], g1, s1, 1, True))

    for wt in (wt2, wt1):
        for j in range(3):
            wt["wT"][j * N : (j + 1) * N, :] = wt["w"][j].T
        wt["w3T"][...] = wt["w"][3].T
    b["turn"][...] = selection(R, R, lambda i: (lambda u, c, v: (v * 2 + c) * 16 + u)(*digits(i, NG, 2, NR)))
    for c in range(2):
        b["gather"][c] = selection(
            R, 2 * R, lambda i: (lambda u, v, p: ((p * NG + u) * 2 + c) * NR + v)(*digits(i, NG, NR, 2))
        )
    for i in range(2):
        back_start(b["upper"][i], wt2["w3T"], s2, i)
        spread_heads(s1["q"][i], s1["qs"].at[i])

    for c in range(2):
        ex_a[c].wait_recv()
        moved = mm(b["swap"][...], b["a_in"][c].reshape(R, N)).astype(bf16).reshape(NR, 2, 16, N)
        for i in range(2):
            b["b_out"][i, :, c] = moved[:, i]
    for i in range(2):
        ex_b[i].start()
        b["b_in"][i, r] = b["b_out"][i, r]

    def turn(i):
        ex_rb[i].wait_recv()
        b["ra_out"][i] = mm(b["turn"][...], b["rb_in"][i].reshape(R, N)).astype(bf16).reshape(NG, 16, N)
        ex_ra[i].start()
        b["ra_in"][i, g] = b["ra_out"][i, g]

    for i in range(2):
        ex_b[i].wait_recv()
        forward(b["b_in"][i].reshape(R, N).astype(f32), wt2["w"], g2, s2, i, False)
        spread_heads(s2["q"][i], s2["qs"].at[i])
        if i == 1:
            turn(0)
        back_heads(s2, i)
        dx = back_input(b["upper"][i], wt2["wT"], g2, s2, i)
        b["rb_out"][i] = dx.astype(bf16).reshape(NR, 2, 16, N)
        ex_rb[i].start()
        b["rb_in"][i, r] = b["rb_out"][i, r]

    def output_weights(s, top):
        return mm(s["combT"][0].astype(bf16), top[0]) + mm(s["combT"][1].astype(bf16), top[1])

    sum_inter.put(3, output_weights(s2, b["upper"]))
    proj = mm(s2["hiddenT"][...], s2["gqkv"][...])
    for j in range(3):
        sum_inter.put(j, proj[:, j * N : (j + 1) * N])
    sum_inter.first()
    turn(1)
    sum_inter.second()

    for i in range(2):
        ex_ra[i].wait_recv()
    came = b["ra_in"][...].reshape(2 * R, N)
    for c in range(2):
        b["top"][c] = mm(b["gather"][c], came).astype(bf16)
    for c in (1, 0):
        back_start(b["top"][c], wt1["w3T"], s1, c)
        if c == 1:
            sum_out.put(0, output_weights(s1, b["top"]))
            sum_out.first()
        back_heads(s1, c)
        if c == 1:
            sum_inter.third()
            sum_out.second()
    proj = mm(s1["hiddenT"][...], s1["gqkv"][...])
    for j in range(3):
        sum_proj.put(j, proj[:, j * N : (j + 1) * N])
    sum_proj.first()
    dx1 = back_input(b["top"][1], wt1["wT"], g1, s1, 1)
    b["tail"][...] = dx1[R // 2 :].astype(bf16)
    tail = copy("tail", 0, b["tail"], b["tail_in"], {"seq": right})
    tail.start()
    sum_proj.second()
    dx0 = back_input(b["top"][0], wt1["wT"], g1, s1, 0)
    sum_inter.fourth()
    sum_out.third()
    sum_proj.third()
    sum_out.fourth()
    sum_inter.fifth()
    tail.wait_recv()
    carried = jnp.where(me > 0, b["tail_in"][...].astype(f32), 0.0)
    gf[0, 0 : R // 2] = (dx0[0 : R // 2] + carried).astype(bf16)
    gf[0, R // 2 :] = (dx0[R // 2 :] + dx1[0 : R // 2]).astype(bf16)
    sum_proj.fourth()
    sum_out.fifth()

    def gain_sum(l, w, gw):
        total = w[0].astype(f32) * gw[0].astype(f32)
        for j in range(1, 3):
            total += w[j].astype(f32) * gw[j].astype(f32)
        rows = jnp.broadcast_to(jnp.sum(total, -1, keepdims=True), (N, 128))
        gg[l : l + 1] = rows.T[0:1] / b["gains"][l : l + 1]

    sum_inter.finish(gw2, 0)
    gain_sum(1, wt2["w"], gw2)
    sum_proj.fifth()
    sum_out.finish(gw1, 3)
    sum_proj.finish(gw1, 0)
    gain_sum(0, wt1["w"], gw1)

    halo.wait_send()
    tail.wait_send()
    for s in (sum_inter, sum_out, sum_proj):
        s.wait_send()
    for ex in Exchange.started:
        ex.wait_send()


def widen(gf, gw1, gw2, gg, gf_out, gw1_out, gw2_out, gg_out):
    gw1_out[...] = gw1[...].astype(f32)
    gw2_out[...] = gw2[...].astype(f32)
    gf_out[...] = gf[...]
    gg_out[...] = gg[...]


def on_device(n_seq, frames, upstream, w1, w2, gains):
    vmem = pl.BlockSpec(memory_space=pltpu.VMEM)
    bufs, sems = comm_scratch()

    def shapes(kind):
        return [
            jax.ShapeDtypeStruct(frames.shape, bf16),
            jax.ShapeDtypeStruct(w1.shape, kind),
            jax.ShapeDtypeStruct(w2.shape, kind),
            jax.ShapeDtypeStruct(gains.shape, f32),
        ]

    found = pl.pallas_call(
        functools.partial(kernel, n_seq),
        in_specs=[pl.BlockSpec(memory_space=pl.ANY)] * 5,
        out_specs=[vmem] * 4,
        out_shape=shapes(bf16),
        scratch_shapes=[
            saved_scratch(),
            saved_scratch(),
            shared_scratch(),
            weight_scratch(),
            weight_scratch(),
            bufs,
            sems,
        ],
        compiler_params=pltpu.CompilerParams(
            collective_id=0, has_side_effects=True, vmem_limit_bytes=56 * 2**20
        ),
        name="block_backward",
    )(frames, upstream, w1, w2, gains)
    return pl.pallas_call(
        widen,
        in_specs=[vmem] * 4,
        out_specs=[vmem] * 4,
        out_shape=shapes(f32),
        compiler_params=pltpu.CompilerParams(vmem_limit_bytes=60 * 2**20),
        name="widen",
    )(*found)


def solution(mesh):
    placed = (P("dp", "seq", None), P("dp", "seq", None, None), P(), P(), P())
    return jax.shard_map(
        functools.partial(on_device, mesh.shape["seq"]),
        mesh=mesh,
        in_specs=placed,
        out_specs=(P("dp", "seq", None), P(), P(), P()),
        check_vma=False,
    )
```

time: 107 us -> 90.9 us (0.85)
  Pallas kernels: 100 us -> 90.1 us
  local copies, waits for them, and re-layouts: 5.5 us -> 0 us
    pallas_call x1 -> x2, Pallas kernels: 100 us -> 90.1 us  [the longest x1 87.4 us: on_device(): pl.pallas_call(functools.partial(kernel, n_seq), in_specs=[pl.BlockSpec(m...]
    unnamed x8 -> x0, local copies, waits for them, and re-layouts: 5.5 us -> none
where the time goes in v2:
time: 90.9 us; the launch traced here: 90.8 us
  Pallas kernels  90.1 us (99%)
    pallas_call x1, Pallas kernels, on_device(): pl.pallas_call(functools.partial(kernel, n_seq), in_specs=[pl.BlockSpec(m...  87.4 us
    pallas_call x1, Pallas kernels, on_device(): pl.pallas_call(widen, in_specs=[vmem] * 4, out_specs=[vmem] * 4, out_shap...  2.68 us

profile of v2, /device:TPU:1, one launch (start us, length us, event | category | flops | bytes accessed | tf_op | source)
XLA Modules:
  0.0 90.8 jit_solution(16245836526911942178)
XLA Ops:
  0.6 87.4 %block_backward.1 = (bf16[1,256,256]{2,1,0:T(8,128)(2,1)}, bf16[4,256,256]{2,1,0:T(8,128)(2,1)}, bf16[4,256,256]{2,1,0:T(8,128)(2,1)}, f32[2,256]{1,0:T(2,128)}) custom-call(bf16[1,256,256]{2,1,0:T(8,128)(2,1)} %frames_hbm.1, bf16[1,2,256,256]{3,2,1,0:T(8,128)(2,1)} %upstream_hbm.1, bf16[4,256,256]{2,1,0:T(8,128)(2,1)} %w1_hbm.1, ...), custom_call_target="tpu_custom_call" | custom-call | tf_op jit(solution)/shard_map/block_backward/pallas_call | solution.py:531
  88.1 2.7 %widen.1 = (bf16[1,256,256]{2,1,0:T(8,128)(2,1)}, f32[4,256,256]{2,1,0:T(8,128)}, f32[4,256,256]{2,1,0:T(8,128)}, f32[2,256]{1,0:T(2,128)}) custom-call(bf16[1,256,256]{2,1,0:T(8,128)(2,1)} %get-tuple-element.8.gf, bf16[4,256,256]{2,1,0:T(8,128)(2,1)} %get-tuple-element.9.gw1, bf16[4,256,256]{2,1,0:T(8,128)(2,1)} %get-tuple-element.10.gw2, ...), custom_call_target="tpu_custom_call" | custom-call | tf_op jit(solution)/shard_map/widen/pallas_call | solution.py:550

commit v3 on v2

--- a/solution.py
+++ b/solution.py
@@ -292,6 +292,20 @@
         def wait_send(self):
             loop(1, self.n, lambda d: self.out(d).wait_send())
 
+    class Single:
+        def __init__(self, out, came):
+            self.out, self.came = out, came
+
+        def start(self):
+            self.out.start()
+            Exchange.started.append(self)
+
+        def wait_recv(self):
+            self.came.wait_recv()
+
+        def wait_send(self):
+            self.out.wait_send()
+
     def far_exchange(name, i):
         out, into = b[name + "_out"], b[name + "_in"]
         return Exchange(name, NG, g, at_far, lambda p: out.at[i, p], lambda p: into.at[i, p], NG * i)
@@ -312,7 +326,8 @@
             every = b[name + "_all"]
             self.pair, self.pair_in, self.every = pair, pair_in, every
             self.xy, self.xy_in, self.z = b[name + "_xy"], b[name + "_xy_in"], b[name + "_z"]
-            self.ex_pair = copy(name + "_pair", 0, pair.at[1 - core], pair_in, other_core)
+            pair_out = copy(name + "_pair", 0, pair.at[1 - core], pair_in, other_core)
+            self.ex_pair = Single(pair_out, pair_out)
             self.ex_xy = Exchange(
                 name + "_xy", NG, xy, at_xy, lambda p: self.xy.at[p], lambda p: self.xy_in.at[p]
             )
@@ -320,8 +335,10 @@
             self.ex_share = Exchange(
                 name + "_share", NG, xy, at_xy, lambda p: every.at[core, xy], lambda p: every.at[core, p]
             )
-            self.ex_last = copy(name + "_last", 0, every.at[core], every.at[core], other_core)
-            self.ex_last_in = copy(name + "_last", 0, every.at[1 - core], every.at[1 - core], other_core)
+            self.ex_last = Single(
+                copy(name + "_last", 0, every.at[core], every.at[core], other_core),
+                copy(name + "_last", 0, every.at[1 - core], every.at[1 - core], other_core),
+            )
 
         def put(self, j, matrix):
             matrix = matrix.astype(bf16)
@@ -361,17 +378,13 @@
             self.ex_last.start()
 
         def finish(self, out, first):
-            self.ex_last_in.wait_recv()
+            self.ex_last.wait_recv()
             for k in range(CORE):
                 for p in range(NG):
                     row, lane = k * 128 + p // 2 * 16, p % 2 * 128
                     for j in range(self.m):
                         out[first + j, row : row + 16, lane : lane + 128] = self.every[k, p, j]
 
-        def wait_send(self):
-            self.ex_pair.wait_send()
-            self.ex_last.wait_send()
-
     sum_inter, sum_out, sum_proj = Sum("inter"), Sum("out"), Sum("proj")
 
     def spread(c, out):
@@ -387,6 +400,7 @@
 
     pl.semaphore_wait(barrier, greetings)
     halo = copy("halo", 0, b["frames"].at[0 : R // 2], b["halo"], {"seq": left})
+    halo = Single(halo, halo)
     halo.start()
     spread(0, out0)
 
@@ -472,6 +486,7 @@
     dx1 = back_input(b["top"][1], wt1["wT"], g1, s1, 1)
     b["tail"][...] = dx1[R // 2 :].astype(bf16)
     tail = copy("tail", 0, b["tail"], b["tail_in"], {"seq": right})
+    tail = Single(tail, tail)
     tail.start()
     sum_proj.second()
     dx0 = back_input(b["top"][0], wt1["wT"], g1, s1, 0)
@@ -501,10 +516,6 @@
     sum_proj.finish(gw1, 0)
     gain_sum(0, wt1["w"], gw1)
 
-    halo.wait_send()
-    tail.wait_send()
-    for s in (sum_inter, sum_out, sum_proj):
-        s.wait_send()
     for ex in Exchange.started:
         ex.wait_send()
 

time: 90.9 us -> 90.8 us (level)
  no operation moved by 1% of the time
where the time goes in v3:
time: 90.8 us; the launch traced here: 90.7 us
  Pallas kernels  90.1 us (99%)
    pallas_call x1, Pallas kernels, on_device(): pl.pallas_call(functools.partial(kernel, n_seq), in_specs=[pl.BlockSpec(m...  87.4 us
    pallas_call x1, Pallas kernels, on_device(): pl.pallas_call(widen, in_specs=[vmem] * 4, out_specs=[vmem] * 4, out_shap...  2.68 us

profile of v3, /device:TPU:1, one launch (start us, length us, event | category | flops | bytes accessed | tf_op | source)
XLA Modules:
  0.0 90.7 jit_solution(6334579684937106915)
XLA Ops:
  0.6 87.4 %block_backward.1 = (bf16[1,256,256]{2,1,0:T(8,128)(2,1)}, bf16[4,256,256]{2,1,0:T(8,128)(2,1)}, bf16[4,256,256]{2,1,0:T(8,128)(2,1)}, f32[2,256]{1,0:T(2,128)}) custom-call(bf16[1,256,256]{2,1,0:T(8,128)(2,1)} %frames_hbm.1, bf16[1,2,256,256]{3,2,1,0:T(8,128)(2,1)} %upstream_hbm.1, bf16[4,256,256]{2,1,0:T(8,128)(2,1)} %w1_hbm.1, ...), custom_call_target="tpu_custom_call" | custom-call | tf_op jit(solution)/shard_map/block_backward/pallas_call | solution.py:542
  88.0 2.7 %widen.1 = (bf16[1,256,256]{2,1,0:T(8,128)(2,1)}, f32[4,256,256]{2,1,0:T(8,128)}, f32[4,256,256]{2,1,0:T(8,128)}, f32[2,256]{1,0:T(2,128)}) custom-call(bf16[1,256,256]{2,1,0:T(8,128)(2,1)} %get-tuple-element.8.gf, bf16[4,256,256]{2,1,0:T(8,128)(2,1)} %get-tuple-element.9.gw1, bf16[4,256,256]{2,1,0:T(8,128)(2,1)} %get-tuple-element.10.gw2, ...), custom_call_target="tpu_custom_call" | custom-call | tf_op jit(solution)/shard_map/widen/pallas_call | solution.py:561

commit v4 on v3

--- a/solution.py
+++ b/solution.py
@@ -33,6 +33,10 @@
     return jnp.where((lane >= D * h) & (lane < D * (h + 1)), 1.0, 0.0).astype(bf16)
 
 
+def tdot(a, b):
+    return lax.dot_general(a, b, (((0,), (0,)), ((), ())), preferred_element_type=f32)
+
+
 def forward(x, w, gain, s, i, want_out):
     cen = x - jnp.mean(x, -1, keepdims=True)
     inv = lax.rsqrt(jnp.mean(cen * cen, -1, keepdims=True) + EPS)
@@ -40,23 +44,21 @@
     s["normed"][i] = normed
     s["inv"][i] = inv
     hidden = (normed * gain).astype(bf16)
-    s["hiddenT"][:, i * R : (i + 1) * R] = hidden.T
+    s["k"][i] = mm(hidden, w[1]).astype(bf16)
     q = mm(hidden, w[0])
+    s["qT"][i] = (q * (C * LOG2E)).astype(bf16).T
     s["q"][i] = q.astype(bf16)
-    s["qT"][i] = (q * (C * LOG2E)).astype(bf16).T
-    k = mm(hidden, w[1]).astype(bf16)
-    s["k"][i] = k
-    s["kT"][i] = k.T
-    v = mm(hidden, w[2]).astype(bf16)
-    s["v"][i] = v
-    s["vT"][i] = v.T
+    s["vT"][i] = mm(hidden, w[2]).astype(bf16).T
     for h in range(H):
         rows = slice(D * h, D * (h + 1))
-        scores = mm(s["k"][i] * head_mask(h), s["qT"][i])
+        scores = mm(s["k"][i, :, rows], s["qT"][i, rows, :])
         p = jnp.exp2(scores - jnp.max(scores, 0, keepdims=True))
-        a = (p * (1.0 / jnp.sum(p, 0, keepdims=True))).astype(bf16)
-        s["A"][i, :, h * R : (h + 1) * R] = a
-        s["combT"][i, rows, :] = mm(s["vT"][i, rows, :], a)
+        s["A"][i, :, h * R : (h + 1) * R] = (p * (1.0 / jnp.sum(p, 0, keepdims=True))).astype(bf16)
+    for h in range(H):
+        rows = slice(D * h, D * (h + 1))
+        s["combT"][i, rows, :] = mm(s["vT"][i, rows, :], s["A"][i, :, h * R : (h + 1) * R])
+    s["kT"][i] = s["k"][i].T
+    s["hiddenT"][:, i * R : (i + 1) * R] = hidden.T
     if want_out:
         return x + mm(s["combT"][i].astype(bf16).T, w[3])
     return None
@@ -77,11 +79,13 @@
     for h in range(H):
         rows = slice(D * h, D * (h + 1))
         cols = slice(h * R, (h + 1) * R)
-        ga = mm(s["v"][i] * head_mask(h), s["gcT"][i])
+        ga = tdot(s["vT"][i, rows, :], s["gcT"][i, rows, :])
         drow = jnp.sum(s["gcT"][i, rows, :].astype(f32) * s["combT"][i, rows, :], 0, keepdims=True)
-        d = (s["A"][i, :, cols].astype(f32) * (ga - drow)).astype(bf16)
-        s["Dm"][:, cols] = d
-        s["gqT"][rows, :] = (mm(s["kT"][i, rows, :], d) * C).astype(bf16)
+        s["Dm"][:, cols] = (s["A"][i, :, cols].astype(f32) * (ga - drow)).astype(bf16)
+    for h in range(H):
+        rows = slice(D * h, D * (h + 1))
+        cols = slice(h * R, (h + 1) * R)
+        s["gqT"][rows, :] = (mm(s["kT"][i, rows, :], s["Dm"][:, cols]) * C).astype(bf16)
     mine = slice(i * R, (i + 1) * R)
     s["gqkv"][mine, 2 * N : 3 * N] = mm(s["A"][i], s["gcs"][i]).astype(bf16)
     s["gqkv"][mine, N : 2 * N] = (mm(s["Dm"][...], s["qs"][i]) * C).astype(bf16)
@@ -112,7 +116,6 @@
         qT=square(bf16),
         k=square(bf16),
         kT=square(bf16),
-        v=square(bf16),
         vT=square(bf16),
         A=pltpu.VMEM((2, R, H * R), bf16),
         combT=square(f32),

time: 90.8 us -> 82.5 us (0.909)
  Pallas kernels: 90.1 us -> 81.8 us
    pallas_call x1, Pallas kernels: 87.4 us -> 79.1 us  [on_device(): pl.pallas_call(functools.partial(kernel, n_seq), in_specs=[pl.BlockSpec(m...]
where the time goes in v4:
time: 82.5 us; the launch traced here: 82.4 us
  Pallas kernels  81.8 us (99%)
    pallas_call x1, Pallas kernels, on_device(): pl.pallas_call(functools.partial(kernel, n_seq), in_specs=[pl.BlockSpec(m...  79.1 us
    pallas_call x1, Pallas kernels, on_device(): pl.pallas_call(widen, in_specs=[vmem] * 4, out_specs=[vmem] * 4, out_shap...  2.68 us

profile of v4, /device:TPU:1, one launch (start us, length us, event | category | flops | bytes accessed | tf_op | source)
XLA Modules:
  0.0 82.4 jit_solution(17017504913110361071)
XLA Ops:
  0.6 79.1 %block_backward.1 = (bf16[1,256,256]{2,1,0:T(8,128)(2,1)}, bf16[4,256,256]{2,1,0:T(8,128)(2,1)}, bf16[4,256,256]{2,1,0:T(8,128)(2,1)}, f32[2,256]{1,0:T(2,128)}) custom-call(bf16[1,256,256]{2,1,0:T(8,128)(2,1)} %frames_hbm.1, bf16[1,2,256,256]{3,2,1,0:T(8,128)(2,1)} %upstream_hbm.1, bf16[4,256,256]{2,1,0:T(8,128)(2,1)} %w1_hbm.1, ...), custom_call_target="tpu_custom_call" | custom-call | tf_op jit(solution)/shard_map/block_backward/pallas_call | solution.py:545
  79.7 2.7 %widen.1 = (bf16[1,256,256]{2,1,0:T(8,128)(2,1)}, f32[4,256,256]{2,1,0:T(8,128)}, f32[4,256,256]{2,1,0:T(8,128)}, f32[2,256]{1,0:T(2,128)}) custom-call(bf16[1,256,256]{2,1,0:T(8,128)(2,1)} %get-tuple-element.8.gf, bf16[4,256,256]{2,1,0:T(8,128)(2,1)} %get-tuple-element.9.gw1, bf16[4,256,256]{2,1,0:T(8,128)(2,1)} %get-tuple-element.10.gw2, ...), custom_call_target="tpu_custom_call" | custom-call | tf_op jit(solution)/shard_map/widen/pallas_call | solution.py:564

commit v5 on v4

--- a/solution.py
+++ b/solution.py
@@ -75,6 +75,10 @@
     spread_heads(gc, s["gcs"].at[i])
 
 
+def back_values(s, i):
+    s["gqkv"][i * R : (i + 1) * R, 2 * N : 3 * N] = mm(s["A"][i], s["gcs"][i]).astype(bf16)
+
+
 def back_heads(s, i):
     for h in range(H):
         rows = slice(D * h, D * (h + 1))
@@ -87,7 +91,6 @@
         cols = slice(h * R, (h + 1) * R)
         s["gqT"][rows, :] = (mm(s["kT"][i, rows, :], s["Dm"][:, cols]) * C).astype(bf16)
     mine = slice(i * R, (i + 1) * R)
-    s["gqkv"][mine, 2 * N : 3 * N] = mm(s["A"][i], s["gcs"][i]).astype(bf16)
     s["gqkv"][mine, N : 2 * N] = (mm(s["Dm"][...], s["qs"][i]) * C).astype(bf16)
     s["gqkv"][mine, 0:N] = s["gqT"][...].T
 
@@ -134,7 +137,7 @@
     return dict(w=pltpu.VMEM((4, N, N), bf16), wT=pltpu.VMEM((3 * N, N), bf16), w3T=pltpu.VMEM((N, N), bf16))
 
 
-SUMS = {"inter": 4, "out": 1, "proj": 3}
+SUMS = {"inter": 4, "early": 2, "late": 2}
 
 
 def comm_scratch():
@@ -180,14 +183,6 @@
     return bufs, sems
 
 
-def loop(lo, hi, f):
-    def step(d, carry):
-        f(d)
-        return carry
-
-    lax.fori_loop(lo, hi, step, 0)
-
-
 def digits(index, *sizes):
     found = []
     for n in reversed(sizes):
@@ -245,19 +240,34 @@
     def greet(device):
         pl.semaphore_signal(barrier, inc=1, device_id=device, device_id_type=MESH)
 
-    loop(1, NG, lambda d: greet(at_far(lax.rem(g + d, NG))))
-    loop(0, ZH, lambda d: greet(at_z(lax.rem(zh + d, ZH) * DP + 1 - dp)))
-    loop(
-        0,
-        (X - 1) * (Y - 1),
-        lambda d: greet(
-            at_xy(lax.rem(x + 1 + lax.div(d, Y - 1), X) * Y + lax.rem(y + 1 + lax.rem(d, Y - 1), Y))
-        ),
-    )
-    loop(1, NR, lambda d: greet(at_near(lax.rem(r + d, NR))))
-    greet({"seq": right})
-    greet({"seq": left})
-    greetings = NG - 1 + ZH + (X - 1) * (Y - 1) + NR - 1 + 2
+    def ring(n):
+        return lambda o: min(o, n - o)
+
+    def pairs(first, n, second, m, weight):
+        offsets = [(i, j) for i in range(n) for j in range(m) if i or j]
+        offsets.sort(key=lambda o: -ring(n)(o[0]) - weight * ring(m)(o[1]))
+        return [
+            (
+                lax.rem(first + i, n) * m + lax.rem(second + j, m),
+                lax.rem(first + n - i, n) * m + lax.rem(second + m - j, m),
+            )
+            for i, j in offsets
+        ]
+
+    far_peers = pairs(x, X, zh, ZH, 2)
+    near_peers = pairs(y, Y, core, CORE, 0.5)
+    xy_peers = pairs(x, X, y, Y, 1)
+    z_peers = [(lax.rem(z + o, Z), lax.rem(z + Z - o, Z)) for o in sorted(range(1, Z), key=lambda o: -ring(Z)(o))]
+
+    greeted = [at_far(p) for p, _ in far_peers]
+    greeted += [at_z(lax.rem(zh + o, ZH) * DP + 1 - dp) for o in (2, 1, 3, 0)]
+    greeted += [
+        at_xy(lax.rem(x + i, X) * Y + lax.rem(y + j, Y)) for i in (2, 1, 3) for j in (2, 1, 3)
+    ]
+    greeted += [at_near(p) for p, _ in near_peers] + [{"seq": right}, {"seq": left}]
+    for device in greeted:
+        greet(device)
+    greetings = len(greeted)
 
     def copy(name, d, src, dst, to):
         return pltpu.make_async_remote_copy(
@@ -272,28 +282,22 @@
     class Exchange:
         started = []
 
-        def __init__(self, name, n, mine, address, src, dst, first=0):
-            self.n = n
-
-            def out(d):
-                peer = lax.rem(mine + d, n)
-                return copy(name, first + d, src(peer), dst(mine), address(peer))
-
-            def came(d):
-                peer = lax.rem(mine + n - d, n)
-                return copy(name, first + d, src(peer), dst(peer), address(peer))
-
-            self.out, self.came = out, came
+        def __init__(self, name, peers, mine, address, src, dst, first=0):
+            self.out = [copy(name, first + i, src(to), dst(mine), address(to)) for i, (to, _) in enumerate(peers)]
+            self.came = [copy(name, first + i, src(of), dst(of), address(of)) for i, (_, of) in enumerate(peers)]
 
         def start(self):
-            loop(1, self.n, lambda d: self.out(d).start())
+            for c in self.out:
+                c.start()
             self.started.append(self)
 
         def wait_recv(self):
-            loop(1, self.n, lambda d: self.came(d).wait_recv())
+            for c in self.came:
+                c.wait_recv()
 
         def wait_send(self):
-            loop(1, self.n, lambda d: self.out(d).wait_send())
+            for c in self.out:
+                c.wait_send()
 
     class Single:
         def __init__(self, out, came):
@@ -311,11 +315,11 @@
 
     def far_exchange(name, i):
         out, into = b[name + "_out"], b[name + "_in"]
-        return Exchange(name, NG, g, at_far, lambda p: out.at[i, p], lambda p: into.at[i, p], NG * i)
+        return Exchange(name, far_peers, g, at_far, lambda p: out.at[i, p], lambda p: into.at[i, p], NG * i)
 
     def near_exchange(name, i):
         out, into = b[name + "_out"], b[name + "_in"]
-        return Exchange(name, NR, r, at_near, lambda p: out.at[i, p], lambda p: into.at[i, p], NR * i)
+        return Exchange(name, near_peers, r, at_near, lambda p: out.at[i, p], lambda p: into.at[i, p], NR * i)
 
     ex_a = [far_exchange("a", c) for c in range(2)]
     ex_b = [near_exchange("b", i) for i in range(2)]
@@ -332,11 +336,11 @@
             pair_out = copy(name + "_pair", 0, pair.at[1 - core], pair_in, other_core)
             self.ex_pair = Single(pair_out, pair_out)
             self.ex_xy = Exchange(
-                name + "_xy", NG, xy, at_xy, lambda p: self.xy.at[p], lambda p: self.xy_in.at[p]
+                name + "_xy", xy_peers, xy, at_xy, lambda p: self.xy.at[p], lambda p: self.xy_in.at[p]
             )
-            self.ex_z = Exchange(name + "_z", Z, z, at_z, lambda p: self.z.at[z], lambda p: self.z.at[p])
+            self.ex_z = Exchange(name + "_z", z_peers, z, at_z, lambda p: self.z.at[z], lambda p: self.z.at[p])
             self.ex_share = Exchange(
-                name + "_share", NG, xy, at_xy, lambda p: every.at[core, xy], lambda p: every.at[core, p]
+                name + "_share", xy_peers, xy, at_xy, lambda p: every.at[core, xy], lambda p: every.at[core, p]
             )
             self.ex_last = Single(
                 copy(name + "_last", 0, every.at[core], every.at[core], other_core),
@@ -388,7 +392,7 @@
                     for j in range(self.m):
                         out[first + j, row : row + 16, lane : lane + 128] = self.every[k, p, j]
 
-    sum_inter, sum_out, sum_proj = Sum("inter"), Sum("out"), Sum("proj")
+    sum_inter, sum_early, sum_late = Sum("inter"), Sum("early"), Sum("late")
 
     def spread(c, out):
         b["a_out"][c] = out.astype(bf16).reshape(NG, 16, N)
@@ -451,6 +455,7 @@
         spread_heads(s2["q"][i], s2["qs"].at[i])
         if i == 1:
             turn(0)
+        back_values(s2, i)
         back_heads(s2, i)
         dx = back_input(b["upper"][i], wt2["wT"], g2, s2, i)
         b["rb_out"][i] = dx.astype(bf16).reshape(NR, 2, 16, N)
@@ -465,45 +470,46 @@
     for j in range(3):
         sum_inter.put(j, proj[:, j * N : (j + 1) * N])
     sum_inter.first()
+    sum_inter.second()
     turn(1)
-    sum_inter.second()
 
     for i in range(2):
         ex_ra[i].wait_recv()
     came = b["ra_in"][...].reshape(2 * R, N)
     for c in range(2):
         b["top"][c] = mm(b["gather"][c], came).astype(bf16)
-    for c in (1, 0):
+    for c in range(2):
         back_start(b["top"][c], wt1["w3T"], s1, c)
-        if c == 1:
-            sum_out.put(0, output_weights(s1, b["top"]))
-            sum_out.first()
-        back_heads(s1, c)
-        if c == 1:
-            sum_inter.third()
-            sum_out.second()
-    proj = mm(s1["hiddenT"][...], s1["gqkv"][...])
-    for j in range(3):
-        sum_proj.put(j, proj[:, j * N : (j + 1) * N])
-    sum_proj.first()
+        back_values(s1, c)
+    sum_early.put(0, mm(s1["hiddenT"][...], s1["gqkv"][:, 2 * N : 3 * N]))
+    sum_early.put(1, output_weights(s1, b["top"]))
+    sum_early.first()
+    back_heads(s1, 1)
+    sum_inter.third()
+    sum_early.second()
+    back_heads(s1, 0)
+    proj = mm(s1["hiddenT"][...], s1["gqkv"][:, 0 : 2 * N])
+    for j in range(2):
+        sum_late.put(j, proj[:, j * N : (j + 1) * N])
+    sum_late.first()
     dx1 = back_input(b["top"][1], wt1["wT"], g1, s1, 1)
     b["tail"][...] = dx1[R // 2 :].astype(bf16)
     tail = copy("tail", 0, b["tail"], b["tail_in"], {"seq": right})
     tail = Single(tail, tail)
     tail.start()
-    sum_proj.second()
+    sum_late.second()
     dx0 = back_input(b["top"][0], wt1["wT"], g1, s1, 0)
     sum_inter.fourth()
-    sum_out.third()
-    sum_proj.third()
-    sum_out.fourth()
+    sum_early.third()
+    sum_late.third()
+    sum_early.fourth()
     sum_inter.fifth()
     tail.wait_recv()
     carried = jnp.where(me > 0, b["tail_in"][...].astype(f32), 0.0)
     gf[0, 0 : R // 2] = (dx0[0 : R // 2] + carried).astype(bf16)
     gf[0, R // 2 :] = (dx0[R // 2 :] + dx1[0 : R // 2]).astype(bf16)
-    sum_proj.fourth()
-    sum_out.fifth()
+    sum_late.fourth()
+    sum_early.fifth()
 
     def gain_sum(l, w, gw):
         total = w[0].astype(f32) * gw[0].astype(f32)
@@ -514,9 +520,9 @@
 
     sum_inter.finish(gw2, 0)
     gain_sum(1, wt2["w"], gw2)
-    sum_proj.fifth()
-    sum_out.finish(gw1, 3)
-    sum_proj.finish(gw1, 0)
+    sum_early.finish(gw1, 2)
+    sum_late.fifth()
+    sum_late.finish(gw1, 0)
     gain_sum(0, wt1["w"], gw1)
 
     for ex in Exchange.started:
@@ -561,10 +567,17 @@
         ),
         name="block_backward",
     )(frames, upstream, w1, w2, gains)
+    step = [
+        pl.BlockSpec((1, R // 4, N), lambda i: (0, i, 0)),
+        pl.BlockSpec((1, N, N), lambda i: (i, 0, 0)),
+        pl.BlockSpec((1, N, N), lambda i: (i, 0, 0)),
+        pl.BlockSpec((2, N), lambda i: (0, 0)),
+    ]
     return pl.pallas_call(
         widen,
-        in_specs=[vmem] * 4,
-        out_specs=[vmem] * 4,
+        grid=(4,),
+        in_specs=step,
+        out_specs=step,
         out_shape=shapes(f32),
         compiler_params=pltpu.CompilerParams(vmem_limit_bytes=60 * 2**20),
         name="widen",

time: 82.5 us -> 80.5 us (0.976)
  Pallas kernels: 81.8 us -> 79.7 us
    pallas_call x1, Pallas kernels: 79.1 us -> 76 us  [on_device(): pl.pallas_call(functools.partial(kernel, n_seq), in_specs=[pl.BlockSpec(m...]
    pallas_call x1, Pallas kernels: 2.68 us -> 3.68 us  [on_device(): pl.pallas_call(widen, grid=(4,), in_specs=step, out_specs=step, out_shape...]
where the time goes in v5:
time: 80.5 us; the launch traced here: 80.3 us
  Pallas kernels  79.7 us (99%)
    pallas_call x1, Pallas kernels, on_device(): pl.pallas_call(functools.partial(kernel, n_seq), in_specs=[pl.BlockSpec(m...  76 us
    pallas_call x1, Pallas kernels, on_device(): pl.pallas_call(widen, grid=(4,), in_specs=step, out_specs=step, out_shape...  3.68 us

profile of v5, /device:TPU:1, one launch (start us, length us, event | category | flops | bytes accessed | tf_op | source)
XLA Modules:
  0.0 80.3 jit_solution(2189190107643247959)
XLA Ops:
  0.6 76.0 %block_backward.1 = (bf16[1,256,256]{2,1,0:T(8,128)(2,1)}, bf16[4,256,256]{2,1,0:T(8,128)(2,1)}, bf16[4,256,256]{2,1,0:T(8,128)(2,1)}, f32[2,256]{1,0:T(2,128)}) custom-call(bf16[1,256,256]{2,1,0:T(8,128)(2,1)} %frames_hbm.1, bf16[1,2,256,256]{3,2,1,0:T(8,128)(2,1)} %upstream_hbm.1, bf16[4,256,256]{2,1,0:T(8,128)(2,1)} %w1_hbm.1, ...), custom_call_target="tpu_custom_call" | custom-call | tf_op jit(solution)/shard_map/block_backward/pallas_call | solution.py:551
  76.6 3.7 %widen.1 = (bf16[1,256,256]{2,1,0:T(8,128)(2,1)}, f32[4,256,256]{2,1,0:T(8,128)}, f32[4,256,256]{2,1,0:T(8,128)}, f32[2,256]{1,0:T(2,128)}) custom-call(bf16[1,256,256]{2,1,0:T(8,128)(2,1)} %get-tuple-element.8.gf, bf16[4,256,256]{2,1,0:T(8,128)(2,1)} %get-tuple-element.9.gw1, bf16[4,256,256]{2,1,0:T(8,128)(2,1)} %get-tuple-element.10.gw2, ...), custom_call_target="tpu_custom_call" | custom-call | tf_op jit(solution)/shard_map/widen/pallas_call | solution.py:576

commit v6 on v5

--- a/solution.py
+++ b/solution.py
@@ -453,8 +453,6 @@
         ex_b[i].wait_recv()
         forward(b["b_in"][i].reshape(R, N).astype(f32), wt2["w"], g2, s2, i, False)
         spread_heads(s2["q"][i], s2["qs"].at[i])
-        if i == 1:
-            turn(0)
         back_values(s2, i)
         back_heads(s2, i)
         dx = back_input(b["upper"][i], wt2["wT"], g2, s2, i)
@@ -470,6 +468,7 @@
     for j in range(3):
         sum_inter.put(j, proj[:, j * N : (j + 1) * N])
     sum_inter.first()
+    turn(0)
     sum_inter.second()
     turn(1)
 
@@ -499,16 +498,16 @@
     tail.start()
     sum_late.second()
     dx0 = back_input(b["top"][0], wt1["wT"], g1, s1, 0)
-    sum_inter.fourth()
     sum_early.third()
     sum_late.third()
+    sum_inter.fourth()
     sum_early.fourth()
-    sum_inter.fifth()
     tail.wait_recv()
     carried = jnp.where(me > 0, b["tail_in"][...].astype(f32), 0.0)
     gf[0, 0 : R // 2] = (dx0[0 : R // 2] + carried).astype(bf16)
     gf[0, R // 2 :] = (dx0[R // 2 :] + dx1[0 : R // 2]).astype(bf16)
     sum_late.fourth()
+    sum_inter.fifth()
     sum_early.fifth()
 
     def gain_sum(l, w, gw):
@@ -529,11 +528,19 @@
         ex.wait_send()
 
 
-def widen(gf, gw1, gw2, gg, gf_out, gw1_out, gw2_out, gg_out):
-    gw1_out[...] = gw1[...].astype(f32)
-    gw2_out[...] = gw2[...].astype(f32)
-    gf_out[...] = gf[...]
-    gg_out[...] = gg[...]
+def widen(gf, gw1, gw2, gg, gf_out, gw1_out, gw2_out, gg_out, narrow, wide, sems_in, sems_out, sems):
+    whole = [pltpu.make_async_copy(gf, gf_out, sems.at[0]), pltpu.make_async_copy(gg, gg_out, sems.at[1])]
+    blocks = [(l, j) for l in range(2) for j in range(4)]
+    came = [pltpu.make_async_copy((gw1, gw2)[l].at[j], narrow.at[l, j], sems_in.at[l, j]) for l, j in blocks]
+    gone = [pltpu.make_async_copy(wide.at[l, j], (gw1_out, gw2_out)[l].at[j], sems_out.at[l, j]) for l, j in blocks]
+    for c in came + whole:
+        c.start()
+    for (l, j), into, out in zip(blocks, came, gone):
+        into.wait()
+        wide[l, j] = narrow[l, j].astype(f32)
+        out.start()
+    for c in gone + whole:
+        c.wait()
 
 
 def on_device(n_seq, frames, upstream, w1, w2, gains):
@@ -567,18 +574,18 @@
         ),
         name="block_backward",
     )(frames, upstream, w1, w2, gains)
-    step = [
-        pl.BlockSpec((1, R // 4, N), lambda i: (0, i, 0)),
-        pl.BlockSpec((1, N, N), lambda i: (i, 0, 0)),
-        pl.BlockSpec((1, N, N), lambda i: (i, 0, 0)),
-        pl.BlockSpec((2, N), lambda i: (0, 0)),
-    ]
     return pl.pallas_call(
         widen,
-        grid=(4,),
-        in_specs=step,
-        out_specs=step,
+        in_specs=[pl.BlockSpec(memory_space=pl.ANY)] * 4,
+        out_specs=[pl.BlockSpec(memory_space=pl.ANY)] * 4,
         out_shape=shapes(f32),
+        scratch_shapes=[
+            pltpu.VMEM((2, 4, N, N), bf16),
+            pltpu.VMEM((2, 4, N, N), f32),
+            pltpu.SemaphoreType.DMA((2, 4)),
+            pltpu.SemaphoreType.DMA((2, 4)),
+            pltpu.SemaphoreType.DMA((2,)),
+        ],
         compiler_params=pltpu.CompilerParams(vmem_limit_bytes=60 * 2**20),
         name="widen",
     )(*found)

time: 80.5 us -> 77.7 us (0.965)
  Pallas kernels: 79.7 us -> 76.8 us
    pallas_call x1, Pallas kernels: 76 us -> 71.5 us  [on_device(): pl.pallas_call(functools.partial(kernel, n_seq), in_specs=[pl.BlockSpec(m...]
    pallas_call x1, Pallas kernels: 3.68 us -> 5.31 us  [on_device(): pl.pallas_call(widen, in_specs=[pl.BlockSpec(memory_space=pl.ANY)] * 4, o...]
where the time goes in v6:
time: 77.7 us; the launch traced here: 77.6 us
  Pallas kernels  76.8 us (99%)
  between operations  0.8 us (1%)
    pallas_call x1, Pallas kernels, on_device(): pl.pallas_call(functools.partial(kernel, n_seq), in_specs=[pl.BlockSpec(m...  71.5 us
    pallas_call x1, Pallas kernels, on_device(): pl.pallas_call(widen, in_specs=[pl.BlockSpec(memory_space=pl.ANY)] * 4, o...  5.31 us

profile of v6, /device:TPU:1, one launch (start us, length us, event | category | flops | bytes accessed | tf_op | source)
XLA Modules:
  0.0 77.6 jit_solution(8856652858387841969)
XLA Ops:
  0.6 71.5 %block_backward.1 = (bf16[1,256,256]{2,1,0:T(8,128)(2,1)}, bf16[4,256,256]{2,1,0:T(8,128)(2,1)}, bf16[4,256,256]{2,1,0:T(8,128)(2,1)}, f32[2,256]{1,0:T(2,128)}) custom-call(bf16[1,256,256]{2,1,0:T(8,128)(2,1)} %frames_hbm.1, bf16[1,2,256,256]{3,2,1,0:T(8,128)(2,1)} %upstream_hbm.1, bf16[4,256,256]{2,1,0:T(8,128)(2,1)} %w1_hbm.1, ...), custom_call_target="tpu_custom_call" | custom-call | tf_op jit(solution)/shard_map/block_backward/pallas_call | solution.py:558
  72.1 5.3 %widen.1 = (bf16[1,256,256]{2,1,0:T(8,128)(2,1)}, f32[4,256,256]{2,1,0:T(8,128)}, f32[4,256,256]{2,1,0:T(8,128)}, f32[2,256]{1,0:T(2,128)}) custom-call(bf16[1,256,256]{2,1,0:T(8,128)(2,1)} %get-tuple-element.8.gf, bf16[4,256,256]{2,1,0:T(8,128)(2,1)} %get-tuple-element.9.gw1, bf16[4,256,256]{2,1,0:T(8,128)(2,1)} %get-tuple-element.10.gw2, ...), custom_call_target="tpu_custom_call" | custom-call | tf_op jit(solution)/shard_map/widen/pallas_call | solution.py:577

commit v7 on v5

--- a/solution.py
+++ b/solution.py
@@ -453,8 +453,6 @@
         ex_b[i].wait_recv()
         forward(b["b_in"][i].reshape(R, N).astype(f32), wt2["w"], g2, s2, i, False)
         spread_heads(s2["q"][i], s2["qs"].at[i])
-        if i == 1:
-            turn(0)
         back_values(s2, i)
         back_heads(s2, i)
         dx = back_input(b["upper"][i], wt2["wT"], g2, s2, i)
@@ -470,6 +468,7 @@
     for j in range(3):
         sum_inter.put(j, proj[:, j * N : (j + 1) * N])
     sum_inter.first()
+    turn(0)
     sum_inter.second()
     turn(1)
 
@@ -499,16 +498,16 @@
     tail.start()
     sum_late.second()
     dx0 = back_input(b["top"][0], wt1["wT"], g1, s1, 0)
-    sum_inter.fourth()
     sum_early.third()
     sum_late.third()
+    sum_inter.fourth()
     sum_early.fourth()
-    sum_inter.fifth()
     tail.wait_recv()
     carried = jnp.where(me > 0, b["tail_in"][...].astype(f32), 0.0)
     gf[0, 0 : R // 2] = (dx0[0 : R // 2] + carried).astype(bf16)
     gf[0, R // 2 :] = (dx0[R // 2 :] + dx1[0 : R // 2]).astype(bf16)
     sum_late.fourth()
+    sum_inter.fifth()
     sum_early.fifth()
 
     def gain_sum(l, w, gw):
@@ -567,17 +566,10 @@
         ),
         name="block_backward",
     )(frames, upstream, w1, w2, gains)
-    step = [
-        pl.BlockSpec((1, R // 4, N), lambda i: (0, i, 0)),
-        pl.BlockSpec((1, N, N), lambda i: (i, 0, 0)),
-        pl.BlockSpec((1, N, N), lambda i: (i, 0, 0)),
-        pl.BlockSpec((2, N), lambda i: (0, 0)),
-    ]
     return pl.pallas_call(
         widen,
-        grid=(4,),
-        in_specs=step,
-        out_specs=step,
+        in_specs=[vmem] * 4,
+        out_specs=[vmem] * 4,
         out_shape=shapes(f32),
         compiler_params=pltpu.CompilerParams(vmem_limit_bytes=60 * 2**20),
         name="widen",

time: 80.5 us -> 75 us (0.932)
  Pallas kernels: 79.7 us -> 74.2 us
    pallas_call x1, Pallas kernels: 76 us -> 71.5 us  [on_device(): pl.pallas_call(functools.partial(kernel, n_seq), in_specs=[pl.BlockSpec(m...]
    pallas_call x1, Pallas kernels: 3.68 us -> 2.68 us  [on_device(): pl.pallas_call(widen, in_specs=[vmem] * 4, out_specs=[vmem] * 4, out_shap...]
where the time goes in v7:
time: 75 us; the launch traced here: 74.8 us
  Pallas kernels  74.2 us (99%)
    pallas_call x1, Pallas kernels, on_device(): pl.pallas_call(functools.partial(kernel, n_seq), in_specs=[pl.BlockSpec(m...  71.5 us
    pallas_call x1, Pallas kernels, on_device(): pl.pallas_call(widen, in_specs=[vmem] * 4, out_specs=[vmem] * 4, out_shap...  2.68 us

profile of v7, /device:TPU:1, one launch (start us, length us, event | category | flops | bytes accessed | tf_op | source)
XLA Modules:
  0.0 74.8 jit_solution(15859165482844865196)
XLA Ops:
  0.6 71.5 %block_backward.1 = (bf16[1,256,256]{2,1,0:T(8,128)(2,1)}, bf16[4,256,256]{2,1,0:T(8,128)(2,1)}, bf16[4,256,256]{2,1,0:T(8,128)(2,1)}, f32[2,256]{1,0:T(2,128)}) custom-call(bf16[1,256,256]{2,1,0:T(8,128)(2,1)} %frames_hbm.1, bf16[1,2,256,256]{3,2,1,0:T(8,128)(2,1)} %upstream_hbm.1, bf16[4,256,256]{2,1,0:T(8,128)(2,1)} %w1_hbm.1, ...), custom_call_target="tpu_custom_call" | custom-call | tf_op jit(solution)/shard_map/block_backward/pallas_call | solution.py:550
  72.1 2.7 %widen.1 = (bf16[1,256,256]{2,1,0:T(8,128)(2,1)}, f32[4,256,256]{2,1,0:T(8,128)}, f32[4,256,256]{2,1,0:T(8,128)}, f32[2,256]{1,0:T(2,128)}) custom-call(bf16[1,256,256]{2,1,0:T(8,128)(2,1)} %get-tuple-element.8.gf, bf16[4,256,256]{2,1,0:T(8,128)(2,1)} %get-tuple-element.9.gw1, bf16[4,256,256]{2,1,0:T(8,128)(2,1)} %get-tuple-element.10.gw2, ...), custom_call_target="tpu_custom_call" | custom-call | tf_op jit(solution)/shard_map/widen/pallas_call | solution.py:569

commit v8 on v7

--- a/solution.py
+++ b/solution.py
@@ -483,8 +483,8 @@
     sum_early.put(0, mm(s1["hiddenT"][...], s1["gqkv"][:, 2 * N : 3 * N]))
     sum_early.put(1, output_weights(s1, b["top"]))
     sum_early.first()
+    sum_inter.third()
     back_heads(s1, 1)
-    sum_inter.third()
     sum_early.second()
     back_heads(s1, 0)
     proj = mm(s1["hiddenT"][...], s1["gqkv"][:, 0 : 2 * N])

time: 75 us -> 74.4 us (level)
  no operation moved by 1% of the time
where the time goes in v8:
time: 74.4 us; the launch traced here: 74.2 us
  Pallas kernels  73.6 us (99%)
    pallas_call x1, Pallas kernels, on_device(): pl.pallas_call(functools.partial(kernel, n_seq), in_specs=[pl.BlockSpec(m...  70.9 us
    pallas_call x1, Pallas kernels, on_device(): pl.pallas_call(widen, in_specs=[vmem] * 4, out_specs=[vmem] * 4, out_shap...  2.68 us

profile of v8, /device:TPU:1, one launch (start us, length us, event | category | flops | bytes accessed | tf_op | source)
XLA Modules:
  0.0 74.2 jit_solution(5975859839762535231)
XLA Ops:
  0.6 70.9 %block_backward.1 = (bf16[1,256,256]{2,1,0:T(8,128)(2,1)}, bf16[4,256,256]{2,1,0:T(8,128)(2,1)}, bf16[4,256,256]{2,1,0:T(8,128)(2,1)}, f32[2,256]{1,0:T(2,128)}) custom-call(bf16[1,256,256]{2,1,0:T(8,128)(2,1)} %frames_hbm.1, bf16[1,2,256,256]{3,2,1,0:T(8,128)(2,1)} %upstream_hbm.1, bf16[4,256,256]{2,1,0:T(8,128)(2,1)} %w1_hbm.1, ...), custom_call_target="tpu_custom_call" | custom-call | tf_op jit(solution)/shard_map/block_backward/pallas_call | solution.py:550
  71.6 2.7 %widen.1 = (bf16[1,256,256]{2,1,0:T(8,128)(2,1)}, f32[4,256,256]{2,1,0:T(8,128)}, f32[4,256,256]{2,1,0:T(8,128)}, f32[2,256]{1,0:T(2,128)}) custom-call(bf16[1,256,256]{2,1,0:T(8,128)(2,1)} %get-tuple-element.8.gf, bf16[4,256,256]{2,1,0:T(8,128)(2,1)} %get-tuple-element.9.gw1, bf16[4,256,256]{2,1,0:T(8,128)(2,1)} %get-tuple-element.10.gw2, ...), custom_call_target="tpu_custom_call" | custom-call | tf_op jit(solution)/shard_map/widen/pallas_call | solution.py:569
